TPU v7x, 256 devices: a whole 4x4x8 slice. The times are simulated.
256 devices in a mesh: band: 64 (over y, z_hi, x), batch: 4 (over z_lo, core).
Axes of the slice: x: 4, y: 4, z: 8 (z_hi: 4, z_lo: 2; z = z_hi * 2 + z_lo), core: 2. Of those that a mesh axis runs over, the one named last changes fastest.
Arguments:
- activations: bfloat16 [4, 64, 256, 768], P('batch', 'band'), may hold values from -36 to 36, as said below
- cotangent: bfloat16 [4, 64, 256, 768], P('batch', 'band'), may hold values from -6 to 6
- qkv_weight: bfloat16 [768, 2304], replicated, as said below
- out_weight: bfloat16 [768, 768], replicated, may hold values from -0.21875 to 0.21875
Outputs:
- grads_in: bfloat16 [4, 64, 256, 768], P('batch', 'band')
- qkv_grad: float32 [768, 2304], P('band')
- out_grad: float32 [768, 768], P('band')
Inputs may be any that keep to these rules, and one draw needn't show every extreme that they name: `activations`: each token's features are random values times a scale of the token and a scale of the feature, both between 0.3 and 3. `qkv_weight`: entries lie within 29 / sqrt(768) in magnitude.
All inputs are finite; a program needn't handle non-finite values.
Results may differ from a plain program's by a relative error of at most 0.014.
Values may be sent and summed in bfloat16 or wider, within the bound.
A program may use at most 64 MiB of HBM per device.

v0:
```python
import math

import jax
import jax.numpy as jnp
from jax import lax
from jax.sharding import PartitionSpec as P

HEADS = 12
HD = 64


EPSILON = 1e-06


def local(activations, cotangent, qkv_weight, out_weight):
    width = activations.shape[-1]
    inputs_col, cot_col = (
        lax.all_to_all(activations, "band", split_axis=2, concat_axis=1, tiled=True),
        lax.all_to_all(cotangent, "band", split_axis=2, concat_axis=1, tiled=True),
    )
    samples, rows, columns, _ = inputs_col.shape
    as_float = inputs_col.astype(jnp.float32)
    inverse = lax.rsqrt(jnp.mean(as_float * as_float, axis=-1, keepdims=True) + EPSILON)
    normed = (as_float * inverse).astype(jnp.bfloat16)
    flat_normed = normed.reshape(-1, width)
    projected = jnp.dot(flat_normed, qkv_weight, preferred_element_type=jnp.float32).astype(
        jnp.bfloat16
    )
    projected = projected.reshape(samples, rows, columns, 3, HEADS, HD)
    queries = projected[:, :, :, 0]
    key_rows = projected[:, :, :, 1]
    value_rows = projected[:, :, :, 2]
    scale_factor = HD ** (-0.5)
    scores = (
        jnp.einsum("bicnh,bjcnh->bcnij", queries, key_rows, preferred_element_type=jnp.float32)
        * scale_factor
    )
    attn_prob = jax.nn.softmax(scores, axis=-1)
    prob_bf = attn_prob.astype(jnp.bfloat16)
    mixed = jnp.einsum(
        "bcnij,bjcnh->bicnh", prob_bf, value_rows, preferred_element_type=jnp.float32
    )
    mixed_bf = mixed.astype(jnp.bfloat16).reshape(-1, width)
    flat_cot = cot_col.reshape(-1, width)
    grad_mixed = jnp.dot(flat_cot, out_weight.T, preferred_element_type=jnp.float32).astype(
        jnp.bfloat16
    )
    grad_mixed = grad_mixed.reshape(samples, rows, columns, HEADS, HD)
    out_part = jnp.dot(mixed_bf.T, flat_cot, preferred_element_type=jnp.float32)
    grad_prob = jnp.einsum(
        "bicnh,bjcnh->bcnij", grad_mixed, value_rows, preferred_element_type=jnp.float32
    )
    grad_score = (
        attn_prob
        * (grad_prob - jnp.sum(attn_prob * grad_prob, axis=-1, keepdims=True))
        * scale_factor
    ).astype(jnp.bfloat16)
    grad_query = jnp.einsum(
        "bcnij,bjcnh->bicnh", grad_score, key_rows, preferred_element_type=jnp.float32
    )
    grad_key = jnp.einsum(
        "bcnij,bicnh->bjcnh", grad_score, queries, preferred_element_type=jnp.float32
    )
    grad_value = jnp.einsum(
        "bcnij,bicnh->bjcnh", prob_bf, grad_mixed, preferred_element_type=jnp.float32
    )
    grad_proj = (
        jnp.stack([grad_query, grad_key, grad_value], axis=3)
        .astype(jnp.bfloat16)
        .reshape(-1, 3 * width)
    )
    qkv_part = jnp.dot(flat_normed.T, grad_proj, preferred_element_type=jnp.float32)
    grad_normed = jnp.dot(grad_proj, qkv_weight.T, preferred_element_type=jnp.float32).reshape(
        samples, rows, columns, width
    )
    centre = jnp.mean(grad_normed * as_float, axis=-1, keepdims=True)
    branch = (inverse * grad_normed - as_float * inverse * inverse * inverse * centre).astype(
        jnp.bfloat16
    )
    branch_rows = lax.all_to_all(branch, "band", split_axis=1, concat_axis=2, tiled=True)
    grads_in = (cotangent.astype(jnp.float32) + branch_rows.astype(jnp.float32)).astype(
        jnp.bfloat16
    )
    total_tokens = (
        activations.shape[0]
        * activations.shape[1]
        * activations.shape[2]
        * lax.axis_size("band")
        * lax.axis_size("batch")
    )
    inverse_root = 1.0 / math.sqrt(total_tokens)
    qkv_part = qkv_part * inverse_root
    out_part = out_part * inverse_root
    qkv_rows, out_rows = (
        lax.psum_scatter(qkv_part, "band", scatter_dimension=0, tiled=True),
        lax.psum_scatter(out_part, "band", scatter_dimension=0, tiled=True),
    )
    qkv_grad, out_grad = (
        lax.psum(qkv_rows.astype(jnp.bfloat16), "batch").astype(jnp.float32),
        lax.psum(out_rows.astype(jnp.bfloat16), "batch").astype(jnp.float32),
    )
    return (grads_in, qkv_grad, out_grad)


def solution(mesh):
    return jax.shard_map(
        local,
        mesh=mesh,
        in_specs=(P("batch", "band", None, None), P("batch", "band", None, None), P(), P()),
        out_specs=(P("batch", "band", None, None), P("band", None), P("band", None)),
        check_vma=False,
    )
```

profile of v0, /device:TPU:1, one launch (start us, length us, event | category | flops | bytes accessed | tf_op | source)
XLA Modules:
  0.0 690.0 jit_solution(17360310071820527181)
XLA Ops:
  7.2 2.6 copy.171
  10.3 4.7 reduce.9
  15.0 2.0 reshape.309
  17.0 15.3 %all-to-all-start = ((bf16[64,2,1536]{2,1,0:T(2,128)(2,1)}), bf16[64,2,1536]{2,1,0:T(2,128)(2,1)}, u32[]{:S(2)}, u32[]{:S(2)}) async-start(bf16[64,2,1536]{2,1,0:T(2,128)(2,1)} %reshape.309), calls=%async_computation | async-start | bytes 786432 | tf_op jit(solution)/shard_map/all_to_all | solution.py:18
  32.4 2.5 copy.170
  34.9 4.7 reduce.10
  39.6 2.0 reshape.311
  41.6 6.5 all-to-all-done
  48.0 6.1 all-to-all-start.1
  54.1 3.5 reshape.310
  57.7 2.0 multiply_reduce_fusion.1
  60.4 2.8 reshape.305
  63.1 5.6 all-to-all-done.1
  68.8 3.5 reshape.312
  72.3 2.8 convolution_convert_fusion.2
  75.1 2.5 reshape.300
  77.5 2.7 copy.103
  80.2 3.2 convolution_convert_fusion
  83.4 4.7 reshape.296
  88.0 4.1 fusion.50
  92.1 1.9 fusion.31
  94.0 4.8 fusion.53
  98.8 5.2 fusion.17
  104.0 5.1 fusion.14
  109.1 3.4 fusion.21
  113.9 2.0 maximum_convert_fusion
  115.9 5.2 copy.105
  121.1 4.8 convert_element_type.146
  125.8 3.5 fusion.23
  129.3 4.1 convolution_multiply_fusion
  134.2 3.3 copy.112
  137.6 2.5 reshape.303
  141.6 2.3 reshape.302
  146.7 6.5 all-to-all-start.2
  153.3 3.2 convolution_multiply_fusion.1
  156.5 304.7 %fusion.49 = (f32[16,2304]{1,0:T(8,128)}, f32[16,768]{1,0:T(8,128)}) fusion(f32[768,2304]{1,0:T(8,128)} %convolution_multiply_fusion, f32[768,768]{1,0:T(8,128)} %convolution_multiply_fusion.1), kind=kCustom, calls=%all-reduce-scatter.2 | all-reduce-scatter fusion | flops 3145729 | bytes 9634816
  468.0 6.3 collective-permute-start.20
  474.3 3.4 collective-permute-start.21
  477.8 8.6 %collective-permute-start.22 = (bf16[16,768]{1,0:T(8,128)(2,1)S(1)}, bf16[16,768]{1,0:T(8,128)(2,1)S(1)}, u32[]{:S(2)}, u32[]{:S(2)}) collective-permute-start(bf16[16,768]{1,0:T(8,128)(2,1)S(1)} %convert.64), channel_id=1, source_target_pairs={{0,28},{4,32},{8,36},{12,40},{16,44},{20,48},{24,52},{28,56},{32,6... | collective-permute-start | bytes 73736
  489.2 5.9 collective-permute-start.15
  495.1 6.7 collective-permute-start.24
  501.8 2.3 collective-permute-start.25
  504.1 6.3 collective-permute-start.26
  513.1 3.9 collective-permute-start.29
  521.8 3.3 collective-permute-start.1
  525.0 4.8 collective-permute-start.2
  529.9 3.4 collective-permute-start.3
  533.3 2.2 collective-permute-start.4
  535.6 4.1 collective-permute-start.5
  539.7 3.6 collective-permute-start.6
  543.4 1.9 collective-permute-start.7
  545.3 2.0 collective-permute-start.8
  547.3 3.5 collective-permute-start.9
  550.8 2.2 collective-permute-start.10
  554.3 24.2 %concatenate.9 = bf16[268,768]{1,0:T(8,128)(2,1)} concatenate(bf16[12,768]{1,0:T(8,128)(2,1)} %copy-done.10, bf16[16,768]{1,0:T(8,128)(2,1)} %copy-done.22, bf16[16,768]{1,0:T(8,128)(2,1)} %copy-done.21, bf16[16,768]{1,0:T(8,128)(2,1)} %copy-done.20, bf16[16,768]{1,0:T(8,128)(2,1)} %copy-done.19, bf16[16,768]{1,0:T(8,128)(2,1)} %copy-done.18, bf16[16,768]{1,0:T(8,128)(2,1)} %copy-done.17, ...), dimensions={0} | concatenate | bytes 847872
  578.5 1.9 collective-permute-start.11
  580.4 1.9 collective-permute-start.12
  582.3 1.9 collective-permute-start.13
  584.2 1.9 collective-permute-start.14
  586.1 1.9 collective-permute-start
  589.5 27.9 %concatenate.8 = bf16[268,2304]{1,0:T(8,128)(2,1)} concatenate(bf16[12,2304]{1,0:T(8,128)(2,1)} %collective-permute-done.15, bf16[16,2304]{1,0:T(8,128)(2,1)} %collective-permute-done.14, bf16[16,2304]{1,0:T(8,128)(2,1)} %collective-permute-done.13, bf16[16,2304]{1,0:T(8,128)(2,1)} %collective-permute-done.12, bf16[16,2304]{1,0:T(8,128)(2,1)} %collective-permute-done.11, ...), dimensions={0} | concatenate | bytes 2543616
  618.9 57.4 %all-reduce.8.cloned.1.call-done = (bf16[12,2304]{1,0:T(8,128)(2,1)}, bf16[12,768]{1,0:T(8,128)(2,1)}) async-done(((bf16[12,2304]{1,0:T(8,128)(2,1)}, bf16[12,768]{1,0:T(8,128)(2,1)}), (bf16[12,2304]{1,0:T(8,128)(2,1)}, bf16[12,768]{1,0:T(8,128)(2,1)})) %all-reduce.8.cloned.1.call-update) | async-done | bytes 73744 | tf_op jit(solution)/shard_map/psum | solution.py:99
  679.2 1.9 reshape.306
  681.2 2.0 add_convert_fusion
  (117 shorter events, 31.3 us)
Async XLA Ops:
  7.2 73.0 %copy-start = (bf16[768,2304]{1,0:T(8,128)(2,1)S(1)}, bf16[768,2304]{1,0:T(8,128)(2,1)}, u32[]{:S(2)}) copy-start(bf16[768,2304]{1,0:T(8,128)(2,1)} %param.6) | copy-start | bytes 10616836
  17.0 31.0 %all-to-all-start = ((bf16[64,2,1536]{2,1,0:T(2,128)(2,1)}), bf16[64,2,1536]{2,1,0:T(2,128)(2,1)}, u32[]{:S(2)}, u32[]{:S(2)}) async-start(bf16[64,2,1536]{2,1,0:T(2,128)(2,1)} %reshape.309), calls=%async_computation | async-start | bytes 786432 | tf_op jit(solution)/shard_map/all_to_all | solution.py:18
  48.0 20.7 %all-to-all-start.1 = ((bf16[64,2,1536]{2,1,0:T(2,128)(2,1)}), bf16[64,2,1536]{2,1,0:T(2,128)(2,1)}, u32[]{:S(2)}, u32[]{:S(2)}) async-start(bf16[64,2,1536]{2,1,0:T(2,128)(2,1)} %reshape.311), calls=%async_computation.1 | async-start | bytes 786432 | tf_op jit(solution)/shard_map/all_to_all | solution.py:19
  88.0 4.1 copy-start.4
  92.1 1.9 copy-start.3
  109.1 3.4 copy-start.5
  109.1 3.4 copy-start.25
  109.1 3.4 copy-start.26
  112.5 1.1 copy-start.6
  112.5 1.4 copy-start.7
  125.8 3.5 copy-start.1
  125.8 3.5 copy-start.2
  146.7 532.5 %all-to-all-start.2 = ((bf16[1,64,4,768]{3,2,0,1:T(4,128)(2,1)}), bf16[1,64,4,768]{3,2,0,1:T(4,128)(2,1)}, u32[]{:S(2)}, u32[]{:S(2)}) async-start(bf16[1,64,4,768]{3,2,0,1:T(4,128)(2,1)} %copy.109), calls=%async_computation.2 | async-start | bytes 786432 | tf_op jit(solution)/shard_map/all_to_all | solution.py:80
  153.2 523.1 %all-reduce.8.cloned.1.call-start = ((), (), s32[]{:S(2)}) async-start(), calls=%async_computation.3 | async-start | bytes 196608 | tf_op jit(solution)/shard_map/psum | solution.py:99
  156.5 396.5 %copy-start.24 = (u32[256]{0:T(256)S(1)}, u32[256]{0:T(256)}, u32[]{:S(2)}) copy-start(u32[256]{0:T(256)} %constant.20) | copy-start | bytes 3076
  462.0 15.8 %collective-permute-start.17 = (bf16[16,768]{1,0:T(8,128)(2,1)S(1)}, bf16[16,768]{1,0:T(8,128)(2,1)S(1)}, u32[]{:S(2)}, u32[]{:S(2)}) collective-permute-start(bf16[16,768]{1,0:T(8,128)(2,1)S(1)} %convert.64), channel_id=1, source_target_pairs={{0,8},{4,12},{8,16},{12,20},{16,24},{20,28},{24,32},{28,36},{32,40... | collective-permute-start | bytes 73736
  463.3 23.1 %collective-permute-start.18 = (bf16[16,768]{1,0:T(8,128)(2,1)S(1)}, bf16[16,768]{1,0:T(8,128)(2,1)S(1)}, u32[]{:S(2)}, u32[]{:S(2)}) collective-permute-start(bf16[16,768]{1,0:T(8,128)(2,1)S(1)} %convert.64), channel_id=1, source_target_pairs={{0,12},{4,16},{8,20},{12,24},{16,28},{20,32},{24,36},{28,40},{32,4... | collective-permute-start | bytes 73736
  465.4 8.9 %collective-permute-start.31 = (bf16[12,768]{1,0:T(8,128)(2,1)S(1)}, bf16[12,768]{1,0:T(8,128)(2,1)S(1)}, u32[]{:S(2)}, u32[]{:S(2)}) collective-permute-start(bf16[12,768]{1,0:T(8,128)(2,1)S(1)} %slice.16), channel_id=1, source_target_pairs={{0,64},{4,68},{8,72},{12,76},{16,80},{20,84},{24,88},{28,92},{32,9... | collective-permute-start | bytes 55304
  466.7 22.5 %collective-permute-start.19 = (bf16[16,768]{1,0:T(8,128)(2,1)S(1)}, bf16[16,768]{1,0:T(8,128)(2,1)S(1)}, u32[]{:S(2)}, u32[]{:S(2)}) collective-permute-start(bf16[16,768]{1,0:T(8,128)(2,1)S(1)} %convert.64), channel_id=1, source_target_pairs={{0,16},{4,20},{8,24},{12,28},{16,32},{20,36},{24,40},{28,44},{32,4... | collective-permute-start | bytes 73736
  468.0 27.1 %collective-permute-start.20 = (bf16[16,768]{1,0:T(8,128)(2,1)S(1)}, bf16[16,768]{1,0:T(8,128)(2,1)S(1)}, u32[]{:S(2)}, u32[]{:S(2)}) collective-permute-start(bf16[16,768]{1,0:T(8,128)(2,1)S(1)} %convert.64), channel_id=1, source_target_pairs={{0,20},{4,24},{8,28},{12,32},{16,36},{20,40},{24,44},{28,48},{32,5... | collective-permute-start | bytes 73736
  474.3 13.9 %copy-start.10 = (bf16[12,768]{1,0:T(8,128)(2,1)}, bf16[12,768]{1,0:T(8,128)(2,1)S(1)}, u32[]{:S(2)}) copy-start(bf16[12,768]{1,0:T(8,128)(2,1)S(1)} %collective-permute-done.31) | copy-start | bytes 55300
  474.3 27.4 %collective-permute-start.21 = (bf16[16,768]{1,0:T(8,128)(2,1)S(1)}, bf16[16,768]{1,0:T(8,128)(2,1)S(1)}, u32[]{:S(2)}, u32[]{:S(2)}) collective-permute-start(bf16[16,768]{1,0:T(8,128)(2,1)S(1)} %convert.64), channel_id=1, source_target_pairs={{0,24},{4,28},{8,32},{12,36},{16,40},{20,44},{24,48},{28,52},{32,5... | collective-permute-start | bytes 73736
  477.8 10.5 %copy-start.8 = (bf16[16,768]{1,0:T(8,128)(2,1)}, bf16[16,768]{1,0:T(8,128)(2,1)S(1)}, u32[]{:S(2)}) copy-start(bf16[16,768]{1,0:T(8,128)(2,1)S(1)} %collective-permute-done.17) | copy-start | bytes 73732
  477.8 26.3 %collective-permute-start.22 = (bf16[16,768]{1,0:T(8,128)(2,1)S(1)}, bf16[16,768]{1,0:T(8,128)(2,1)S(1)}, u32[]{:S(2)}, u32[]{:S(2)}) collective-permute-start(bf16[16,768]{1,0:T(8,128)(2,1)S(1)} %convert.64), channel_id=1, source_target_pairs={{0,28},{4,32},{8,36},{12,40},{16,44},{20,48},{24,52},{28,56},{32,6... | collective-permute-start | bytes 73736
  486.4 1.9 copy-start.9
  486.4 24.1 %collective-permute-start.23 = (bf16[16,768]{1,0:T(8,128)(2,1)S(1)}, bf16[16,768]{1,0:T(8,128)(2,1)S(1)}, u32[]{:S(2)}, u32[]{:S(2)}) collective-permute-start(bf16[16,768]{1,0:T(8,128)(2,1)S(1)} %convert.64), channel_id=1, source_target_pairs={{0,32},{4,36},{8,40},{12,44},{16,48},{20,52},{24,56},{28,60},{32,6... | collective-permute-start | bytes 73736
  489.2 46.4 %copy-start.11 = (bf16[16,768]{1,0:T(8,128)(2,1)}, bf16[16,768]{1,0:T(8,128)(2,1)S(1)}, u32[]{:S(2)}) copy-start(bf16[16,768]{1,0:T(8,128)(2,1)S(1)} %collective-permute-done.19) | copy-start | bytes 73732
  489.2 46.4 %collective-permute-start.15 = (bf16[12,2304]{1,0:T(8,128)(2,1)S(1)}, bf16[12,2304]{1,0:T(8,128)(2,1)}, u32[]{:S(2)}, u32[]{:S(2)}) collective-permute-start(bf16[12,2304]{1,0:T(8,128)(2,1)S(1)} %slice.15), channel_id=1, source_target_pairs={{0,64},{4,68},{8,72},{12,76},{16,80},{20,84},{24,88},{28,92},{32,9... | collective-permute-start | bytes 165896
  495.1 44.6 %copy-start.12 = (bf16[16,768]{1,0:T(8,128)(2,1)}, bf16[16,768]{1,0:T(8,128)(2,1)S(1)}, u32[]{:S(2)}) copy-start(bf16[16,768]{1,0:T(8,128)(2,1)S(1)} %collective-permute-done.20) | copy-start | bytes 73732
  495.1 16.7 %collective-permute-start.24 = (bf16[16,768]{1,0:T(8,128)(2,1)S(1)}, bf16[16,768]{1,0:T(8,128)(2,1)S(1)}, u32[]{:S(2)}, u32[]{:S(2)}) collective-permute-start(bf16[16,768]{1,0:T(8,128)(2,1)S(1)} %convert.64), channel_id=1, source_target_pairs={{0,36},{4,40},{8,44},{12,48},{16,52},{20,56},{24,60},{28,64},{32,6... | collective-permute-start | bytes 73736
  501.8 37.9 %copy-start.13 = (bf16[16,768]{1,0:T(8,128)(2,1)}, bf16[16,768]{1,0:T(8,128)(2,1)S(1)}, u32[]{:S(2)}) copy-start(bf16[16,768]{1,0:T(8,128)(2,1)S(1)} %collective-permute-done.21) | copy-start | bytes 73732
  501.8 11.3 %collective-permute-start.25 = (bf16[16,768]{1,0:T(8,128)(2,1)S(1)}, bf16[16,768]{1,0:T(8,128)(2,1)S(1)}, u32[]{:S(2)}, u32[]{:S(2)}) collective-permute-start(bf16[16,768]{1,0:T(8,128)(2,1)S(1)} %convert.64), channel_id=1, source_target_pairs={{0,40},{4,44},{8,48},{12,52},{16,56},{20,60},{24,64},{28,68},{32,7... | collective-permute-start | bytes 73736
  504.1 39.3 %copy-start.14 = (bf16[16,768]{1,0:T(8,128)(2,1)}, bf16[16,768]{1,0:T(8,128)(2,1)S(1)}, u32[]{:S(2)}) copy-start(bf16[16,768]{1,0:T(8,128)(2,1)S(1)} %collective-permute-done.22) | copy-start | bytes 73732
  504.1 12.9 %collective-permute-start.26 = (bf16[16,768]{1,0:T(8,128)(2,1)S(1)}, bf16[16,768]{1,0:T(8,128)(2,1)S(1)}, u32[]{:S(2)}, u32[]{:S(2)}) collective-permute-start(bf16[16,768]{1,0:T(8,128)(2,1)S(1)} %convert.64), channel_id=1, source_target_pairs={{0,44},{4,48},{8,52},{12,56},{16,60},{20,64},{24,68},{28,72},{32,7... | collective-permute-start | bytes 73736
  510.4 32.9 %copy-start.15 = (bf16[16,768]{1,0:T(8,128)(2,1)}, bf16[16,768]{1,0:T(8,128)(2,1)S(1)}, u32[]{:S(2)}) copy-start(bf16[16,768]{1,0:T(8,128)(2,1)S(1)} %collective-permute-done.23) | copy-start | bytes 73732
  510.5 7.8 %collective-permute-start.27 = (bf16[16,768]{1,0:T(8,128)(2,1)S(1)}, bf16[16,768]{1,0:T(8,128)(2,1)S(1)}, u32[]{:S(2)}, u32[]{:S(2)}) collective-permute-start(bf16[16,768]{1,0:T(8,128)(2,1)S(1)} %convert.64), channel_id=1, source_target_pairs={{0,48},{4,52},{8,56},{12,60},{16,64},{20,68},{24,72},{28,76},{32,8... | collective-permute-start | bytes 73736
  511.8 6.5 copy-start.16
  511.8 10.0 %collective-permute-start.28 = (bf16[16,768]{1,0:T(8,128)(2,1)S(1)}, bf16[16,768]{1,0:T(8,128)(2,1)S(1)}, u32[]{:S(2)}, u32[]{:S(2)}) collective-permute-start(bf16[16,768]{1,0:T(8,128)(2,1)S(1)} %convert.64), channel_id=1, source_target_pairs={{0,52},{4,56},{8,60},{12,64},{16,68},{20,72},{24,76},{28,80},{32,8... | collective-permute-start | bytes 73736
  513.1 5.2 copy-start.17
  513.1 12.0 %collective-permute-start.29 = (bf16[16,768]{1,0:T(8,128)(2,1)S(1)}, bf16[16,768]{1,0:T(8,128)(2,1)S(1)}, u32[]{:S(2)}, u32[]{:S(2)}) collective-permute-start(bf16[16,768]{1,0:T(8,128)(2,1)S(1)} %convert.64), channel_id=1, source_target_pairs={{0,56},{4,60},{8,64},{12,68},{16,72},{20,76},{24,80},{28,84},{32,8... | collective-permute-start | bytes 73736
  517.0 1.3 copy-start.18
  517.0 12.9 %collective-permute-start.30 = (bf16[16,768]{1,0:T(8,128)(2,1)S(1)}, bf16[16,768]{1,0:T(8,128)(2,1)S(1)}, u32[]{:S(2)}, u32[]{:S(2)}) collective-permute-start(bf16[16,768]{1,0:T(8,128)(2,1)S(1)} %convert.64), channel_id=1, source_target_pairs={{0,60},{4,64},{8,68},{12,72},{16,76},{20,80},{24,84},{28,88},{32,9... | collective-permute-start | bytes 73736
  518.3 0.6 copy-start.19
  518.9 14.4 %collective-permute-start.16 = (bf16[16,768]{1,0:T(8,128)(2,1)S(1)}, bf16[16,768]{1,0:T(8,128)(2,1)S(1)}, u32[]{:S(2)}, u32[]{:S(2)}) collective-permute-start(bf16[16,768]{1,0:T(8,128)(2,1)S(1)} %convert.64), channel_id=1, source_target_pairs={{0,4},{4,8},{8,12},{12,16},{16,20},{20,24},{24,28},{28,32},{32,36}... | collective-permute-start | bytes 73736
  521.8 23.5 %copy-start.20 = (bf16[16,768]{1,0:T(8,128)(2,1)}, bf16[16,768]{1,0:T(8,128)(2,1)S(1)}, u32[]{:S(2)}) copy-start(bf16[16,768]{1,0:T(8,128)(2,1)S(1)} %collective-permute-done.28) | copy-start | bytes 73732
  521.8 17.9 %collective-permute-start.1 = (bf16[16,2304]{1,0:T(8,128)(2,1)}, bf16[16,2304]{1,0:T(8,128)(2,1)}, u32[]{:S(2)}, u32[]{:S(2)}) collective-permute-start(bf16[16,2304]{1,0:T(8,128)(2,1)} %convert.63), channel_id=1, source_target_pairs={{0,8},{4,12},{8,16},{12,20},{16,24},{20,28},{24,32},{28,36},{32,40... | collective-permute-start | bytes 221192
  525.0 20.3 %copy-start.21 = (bf16[16,768]{1,0:T(8,128)(2,1)}, bf16[16,768]{1,0:T(8,128)(2,1)S(1)}, u32[]{:S(2)}) copy-start(bf16[16,768]{1,0:T(8,128)(2,1)S(1)} %collective-permute-done.29) | copy-start | bytes 73732
  525.0 18.3 %collective-permute-start.2 = (bf16[16,2304]{1,0:T(8,128)(2,1)}, bf16[16,2304]{1,0:T(8,128)(2,1)}, u32[]{:S(2)}, u32[]{:S(2)}) collective-permute-start(bf16[16,2304]{1,0:T(8,128)(2,1)} %convert.63), channel_id=1, source_target_pairs={{0,12},{4,16},{8,20},{12,24},{16,28},{20,32},{24,36},{28,40},{32,4... | collective-permute-start | bytes 221192
  529.9 17.4 %copy-start.22 = (bf16[16,768]{1,0:T(8,128)(2,1)}, bf16[16,768]{1,0:T(8,128)(2,1)S(1)}, u32[]{:S(2)}) copy-start(bf16[16,768]{1,0:T(8,128)(2,1)S(1)} %collective-permute-done.30) | copy-start | bytes 73732
  529.9 15.4 %collective-permute-start.3 = (bf16[16,2304]{1,0:T(8,128)(2,1)}, bf16[16,2304]{1,0:T(8,128)(2,1)}, u32[]{:S(2)}, u32[]{:S(2)}) collective-permute-start(bf16[16,2304]{1,0:T(8,128)(2,1)} %convert.63), channel_id=1, source_target_pairs={{0,16},{4,20},{8,24},{12,28},{16,32},{20,36},{24,40},{28,44},{32,4... | collective-permute-start | bytes 221192
  533.3 14.0 %copy-start.23 = (bf16[16,768]{1,0:T(8,128)(2,1)}, bf16[16,768]{1,0:T(8,128)(2,1)S(1)}, u32[]{:S(2)}) copy-start(bf16[16,768]{1,0:T(8,128)(2,1)S(1)} %collective-permute-done.16) | copy-start | bytes 73732
  533.3 14.0 %collective-permute-start.4 = (bf16[16,2304]{1,0:T(8,128)(2,1)}, bf16[16,2304]{1,0:T(8,128)(2,1)}, u32[]{:S(2)}, u32[]{:S(2)}) collective-permute-start(bf16[16,2304]{1,0:T(8,128)(2,1)} %convert.63), channel_id=1, source_target_pairs={{0,20},{4,24},{8,28},{12,32},{16,36},{20,40},{24,44},{28,48},{32,5... | collective-permute-start | bytes 221192
  535.6 15.2 %collective-permute-start.5 = (bf16[16,2304]{1,0:T(8,128)(2,1)}, bf16[16,2304]{1,0:T(8,128)(2,1)}, u32[]{:S(2)}, u32[]{:S(2)}) collective-permute-start(bf16[16,2304]{1,0:T(8,128)(2,1)} %convert.63), channel_id=1, source_target_pairs={{0,24},{4,28},{8,32},{12,36},{16,40},{20,44},{24,48},{28,52},{32,5... | collective-permute-start | bytes 221192
  539.7 38.8 %collective-permute-start.6 = (bf16[16,2304]{1,0:T(8,128)(2,1)}, bf16[16,2304]{1,0:T(8,128)(2,1)}, u32[]{:S(2)}, u32[]{:S(2)}) collective-permute-start(bf16[16,2304]{1,0:T(8,128)(2,1)} %convert.63), channel_id=1, source_target_pairs={{0,28},{4,32},{8,36},{12,40},{16,44},{20,48},{24,52},{28,56},{32,6... | collective-permute-start | bytes 221192
  543.4 37.0 %collective-permute-start.7 = (bf16[16,2304]{1,0:T(8,128)(2,1)}, bf16[16,2304]{1,0:T(8,128)(2,1)}, u32[]{:S(2)}, u32[]{:S(2)}) collective-permute-start(bf16[16,2304]{1,0:T(8,128)(2,1)} %convert.63), channel_id=1, source_target_pairs={{0,32},{4,36},{8,40},{12,44},{16,48},{20,52},{24,56},{28,60},{32,6... | collective-permute-start | bytes 221192
  545.3 37.0 %collective-permute-start.8 = (bf16[16,2304]{1,0:T(8,128)(2,1)}, bf16[16,2304]{1,0:T(8,128)(2,1)}, u32[]{:S(2)}, u32[]{:S(2)}) collective-permute-start(bf16[16,2304]{1,0:T(8,128)(2,1)} %convert.63), channel_id=1, source_target_pairs={{0,36},{4,40},{8,44},{12,48},{16,52},{20,56},{24,60},{28,64},{32,6... | collective-permute-start | bytes 221192
  547.3 36.9 %collective-permute-start.9 = (bf16[16,2304]{1,0:T(8,128)(2,1)}, bf16[16,2304]{1,0:T(8,128)(2,1)}, u32[]{:S(2)}, u32[]{:S(2)}) collective-permute-start(bf16[16,2304]{1,0:T(8,128)(2,1)} %convert.63), channel_id=1, source_target_pairs={{0,40},{4,44},{8,48},{12,52},{16,56},{20,60},{24,64},{28,68},{32,7... | collective-permute-start | bytes 221192
  550.8 35.3 %collective-permute-start.10 = (bf16[16,2304]{1,0:T(8,128)(2,1)}, bf16[16,2304]{1,0:T(8,128)(2,1)}, u32[]{:S(2)}, u32[]{:S(2)}) collective-permute-start(bf16[16,2304]{1,0:T(8,128)(2,1)} %convert.63), channel_id=1, source_target_pairs={{0,44},{4,48},{8,52},{12,56},{16,60},{20,64},{24,68},{28,72},{32,7... | collective-permute-start | bytes 221192
  578.5 11.0 %collective-permute-start.11 = (bf16[16,2304]{1,0:T(8,128)(2,1)}, bf16[16,2304]{1,0:T(8,128)(2,1)}, u32[]{:S(2)}, u32[]{:S(2)}) collective-permute-start(bf16[16,2304]{1,0:T(8,128)(2,1)} %convert.63), channel_id=1, source_target_pairs={{0,48},{4,52},{8,56},{12,60},{16,64},{20,68},{24,72},{28,76},{32,8... | collective-permute-start | bytes 221192
  580.4 9.1 %collective-permute-start.12 = (bf16[16,2304]{1,0:T(8,128)(2,1)}, bf16[16,2304]{1,0:T(8,128)(2,1)}, u32[]{:S(2)}, u32[]{:S(2)}) collective-permute-start(bf16[16,2304]{1,0:T(8,128)(2,1)} %convert.63), channel_id=1, source_target_pairs={{0,52},{4,56},{8,60},{12,64},{16,68},{20,72},{24,76},{28,80},{32,8... | collective-permute-start | bytes 221192
  582.3 7.1 %collective-permute-start.13 = (bf16[16,2304]{1,0:T(8,128)(2,1)}, bf16[16,2304]{1,0:T(8,128)(2,1)}, u32[]{:S(2)}, u32[]{:S(2)}) collective-permute-start(bf16[16,2304]{1,0:T(8,128)(2,1)} %convert.63), channel_id=1, source_target_pairs={{0,56},{4,60},{8,64},{12,68},{16,72},{20,76},{24,80},{28,84},{32,8... | collective-permute-start | bytes 221192
  584.2 5.2 collective-permute-start.14
  586.1 3.3 collective-permute-start
Sparse Core Ops, SparseCore 0:
  619.1 57.1 all-reduce.7
where the time goes:
time: 695 us; the launch traced here: 690 us
  blocking collectives  305 us (44%)
  starting transfers between devices  124 us (18%)
  local copies, waits for them, and re-layouts  116 us (17%)
  waiting for transfers between devices  69.6 us (10%)
  matrix products  37.7 us (5%)
  other arithmetic  22.4 us (3%)
  between operations  15.1 us (2%)
    unnamed x1, blocking collectives  305 us
    unnamed x32, starting transfers between devices  96.2 us
    unnamed x66, local copies, waits for them, and re-layouts  72.7 us
    psum x1, waiting for transfers between devices, local(): lax.psum(qkv_rows.astype(jnp.bfloat16), 'batch').astype(jnp.float32)  57.4 us
    all_to_all x1, starting transfers between devices, local(): lax.all_to_all(activations, 'band', split_axis=2, concat_axis=1, tiled=True)  15.3 us
  transfers between devices with their start and end apart: 36, of which 3 were waited for; matrix products, arithmetic and copies ran while one was open for 56% of the time, Pallas kernels for 0%

commit v1 on v0

v1 whole, which is shorter than its diff:
```python
import functools
import math

import jax
import jax.numpy as jnp
import numpy as np
from jax import lax
from jax.experimental import pallas as pl
from jax.experimental.pallas import tpu as pltpu
from jax.sharding import PartitionSpec as P

HEADS = 12
HD = 64
EPSILON = 1e-06
MESH = pl.DeviceIdType.MESH
BF = jnp.bfloat16
F32 = jnp.float32
GROUP = 2


def one_hot(rows, cols, index):
    o = lax.broadcasted_iota(jnp.int32, (rows, cols), 0)
    i = lax.broadcasted_iota(jnp.int32, (rows, cols), 1)
    return jnp.where(index(o) == i, 1.0, 0.0).astype(BF)


def dot(a, b, ca=1, cb=0):
    return lax.dot_general(a, b, (((ca,), (cb,)), ((), ())), preferred_element_type=F32)


def place():
    band = lax.axis_index("band")
    batch = lax.axis_index("batch")
    return band, batch, band // 16, (band // 4) % 4, band % 4, batch // 2, batch % 2


def band_peer(k, y, zh, x):
    return ((y + k // 16) % 4) * 16 + ((zh + (k // 4) % 4) % 4) * 4 + (x + k % 4) % 4


def exchange_in(act_ref, cot_ref, x_ref, c_ref, send, recv, ssem, rsem):
    band, batch, y, zh, x, zl, core = place()
    barrier = pltpu.get_barrier_semaphore()

    def greet(k, _):
        pl.semaphore_signal(barrier, 1, device_id=(band_peer(k, y, zh, x), batch), device_id_type=MESH)
        return 0

    lax.fori_loop(1, 64, greet, 0)
    perm = one_hot(256, 256, lambda o: ((o & 15) >> 2) * 64 + (o >> 4) * 4 + (o & 3))
    for g in range(4):
        rows = pl.ds(g * 64, 64)
        stack = jnp.concatenate(
            [act_ref[rows, :384], act_ref[rows, 384:], cot_ref[rows, :384], cot_ref[rows, 384:]], axis=0
        )
        send[pl.ds(g * 16, 16)] = dot(perm, stack).astype(BF).reshape(16, 16, 384)
    pl.semaphore_wait(barrier, 63)

    def push(k, _):
        peer = band_peer(k, y, zh, x)
        pltpu.make_async_remote_copy(
            src_ref=send.at[peer],
            dst_ref=recv.at[band],
            send_sem=ssem,
            recv_sem=rsem,
            device_id=(peer, batch),
            device_id_type=MESH,
        ).start()
        return 0

    lax.fori_loop(1, 64, push, 0)
    recv[band] = send[band]
    pltpu.make_async_copy(recv.at[pl.ds(0, 63)], recv.at[pl.ds(0, 63)], rsem).wait()
    back = one_hot(256, 256, lambda o: ((o & 15) << 4) + ((o >> 6) << 2) + ((o >> 4) & 3))
    for blk in range(4):
        got = recv[pl.ds(blk * 16, 16)].reshape(256, 384)
        out = dot(back, got).astype(BF)
        for t in range(4):
            rows = pl.ds(t * 64 + blk * 16, 16)
            x_ref[rows, :384] = out[t * 16 : t * 16 + 16]
            x_ref[rows, 384:] = out[64 + t * 16 : 64 + t * 16 + 16]
            c_ref[rows, :384] = out[128 + t * 16 : 128 + t * 16 + 16]
            c_ref[rows, 384:] = out[192 + t * 16 : 192 + t * 16 + 16]
    pltpu.make_async_copy(send.at[pl.ds(0, 63)], send.at[pl.ds(0, 63)], ssem).wait()


def attend(x_ref, c_ref, wqkv_ref, wout_ref, normed_ref, gp_ref, mixed_ref, branch_ref, proj, gm):
    as_float = x_ref[...].astype(F32)
    inverse = lax.rsqrt(jnp.mean(as_float * as_float, axis=-1, keepdims=True) + EPSILON)
    normed_ref[...] = (as_float * inverse).astype(BF)
    proj[...] = dot(normed_ref[...], wqkv_ref[...]).astype(BF)
    gm[...] = dot(c_ref[...], wout_ref[...], 1, 1).astype(BF)
    scale = HD ** (-0.5)
    wide = GROUP * HD
    lane = lax.broadcasted_iota(jnp.int32, (1, wide), 1) // HD
    masks = [lane == g for g in range(GROUP)]

    def spread(v):
        zero = jnp.zeros_like(v)
        return jnp.concatenate([jnp.where(m, v, zero) for m in masks], axis=0)

    def gather(r):
        out = r[0:64]
        for g in range(1, GROUP):
            out = jnp.where(masks[g], r[g * 64 : g * 64 + 64], out)
        return out

    for c in range(4):
        rows = pl.ds(c * 64, 64)
        for h in range(HEADS // GROUP):
            at = h * wide
            q = proj[rows, at : at + wide]
            k = proj[rows, 768 + at : 768 + at + wide]
            v = proj[rows, 1536 + at : 1536 + at + wide]
            g = gm[rows, at : at + wide]
            qs, gs = spread(q), spread(g)
            s = dot(k, qs, 1, 1) * scale
            e = jnp.exp(s - jnp.max(s, axis=0, keepdims=True))
            p = e / jnp.sum(e, axis=0, keepdims=True)
            pb = p.astype(BF)
            dp = dot(v, gs, 1, 1)
            ds = (p * (dp - jnp.sum(p * dp, axis=0, keepdims=True)) * scale).astype(BF)
            mixed_ref[rows, at : at + wide] = gather(dot(pb, v, 0, 0)).astype(BF)
            gp_ref[rows, at : at + wide] = gather(dot(ds, k, 0, 0)).astype(BF)
            gp_ref[rows, 768 + at : 768 + at + wide] = dot(ds, qs).astype(BF)
            gp_ref[rows, 1536 + at : 1536 + at + wide] = dot(pb, gs).astype(BF)
    gn = dot(gp_ref[...], wqkv_ref[...], 1, 1)
    xf = x_ref[...].astype(F32)
    centre = jnp.mean(gn * xf, axis=-1, keepdims=True)
    branch_ref[...] = (inverse * gn - xf * (inverse * inverse * inverse * centre)).astype(BF)


def reduce_out(
    normed_ref, gp_ref, mixed_ref, ccol_ref, branch_ref, cot_ref, order_ref,
    gin_ref, gqkv_ref, gout_ref,
    nfull, mfull, ghalf, chalf, bsend, brecv, ga, gb, ra, rb, sa, sb, ra2, rb2, tz, rz, tl, rl, tc, rc,
    fsend, frecv, bssem, brsem, ssem, rsem,
):
    band, batch, y, zh, x, zl, core = place()
    barrier = pltpu.get_barrier_semaphore()
    other = (band, zl * 2 + 1 - core)
    across = (band, (1 - zl) * 2 + core)

    def greet(k, _):
        pl.semaphore_signal(barrier, 1, device_id=(band_peer(k, y, zh, x), batch), device_id_type=MESH)
        return 0

    lax.fori_loop(1, 64, greet, 0)
    pl.semaphore_signal(barrier, 1, device_id=other, device_id_type=MESH)
    pl.semaphore_signal(barrier, 1, device_id=across, device_id_type=MESH)
    perm = one_hot(256, 192, lambda o: jnp.where((o & 15) < 12, ((o & 15) >> 2) * 64 + (o & 3) * 16 + (o >> 4), -1))
    for blk in range(4):
        stack = jnp.concatenate(
            [branch_ref[pl.ds(t * 64 + blk * 16, 16), p * 256 : p * 256 + 256] for p in range(3) for t in range(4)],
            axis=0,
        )
        bsend[pl.ds(blk * 16, 16)] = dot(perm, stack).astype(BF).reshape(16, 16, 256)
    pl.semaphore_wait(barrier, 65)

    mine = pl.ds(pl.multiple_of(core * 256, 256), 256)
    theirs_q = pl.ds(pl.multiple_of((1 - core) * 1152, 128), 1152)
    theirs_c = pl.ds(pl.multiple_of((1 - core) * 384, 128), 384)
    own_q = pl.ds(pl.multiple_of(core * 1152, 128), 1152)
    own_c = pl.ds(pl.multiple_of(core * 384, 128), 384)

    def remote(src, dst, s, r, to):
        return pltpu.make_async_remote_copy(
            src_ref=src, dst_ref=dst, send_sem=s, recv_sem=r, device_id=to, device_id_type=MESH
        )

    factors = [
        remote(normed_ref, nfull.at[mine], fsend.at[0], frecv.at[0], other),
        remote(gp_ref.at[:, theirs_q], ghalf.at[mine], fsend.at[1], frecv.at[1], other),
        remote(mixed_ref, mfull.at[mine], fsend.at[2], frecv.at[2], other),
        remote(ccol_ref.at[:, theirs_c], chalf.at[mine], fsend.at[3], frecv.at[3], other),
    ]
    for f in factors:
        f.start()

    def push(k, _):
        peer = band_peer(k, y, zh, x)
        remote(bsend.at[peer], brecv.at[band], bssem, brsem, (peer, batch)).start()
        return 0

    lax.fori_loop(1, 64, push, 0)
    brecv[band] = bsend[band]
    nfull[mine] = normed_ref[...]
    ghalf[mine] = gp_ref[:, own_q]
    mfull[mine] = mixed_ref[...]
    chalf[mine] = ccol_ref[:, own_c]
    for f in factors:
        f.wait()
    nt = dot(order_ref[...], nfull[...], 1, 1).astype(BF)
    mt = dot(order_ref[...], mfull[...], 1, 1).astype(BF)
    for i in range(4):
        q = dot(nt[i * 192 : i * 192 + 192], ghalf[...]).astype(BF)
        o = dot(mt[i * 192 : i * 192 + 192], chalf[...]).astype(BF)
        for j in range(4):
            ga[j, i] = q[j * 48 : j * 48 + 48, :768]
            gb[i, j, :, :384] = q[j * 48 : j * 48 + 48, 768:]
            gb[i, j, :, 384:] = o[j * 48 : j * 48 + 48]

    def x_peer(d):
        return (y * 16 + zh * 4 + (x + d) % 4, batch)

    def y_peer(d):
        return (((y + d) % 4) * 16 + zh * 4 + x, batch)

    def z_peer(d):
        return (y * 16 + ((zh + d) % 4) * 4 + x, batch)

    copies = []
    for d in range(1, 4):
        copies.append(remote(ga.at[(x + d) % 4], ra.at[d - 1], ssem.at[d - 1], rsem.at[d - 1], x_peer(d)))
        copies.append(remote(gb.at[(y + d) % 4], rb.at[d - 1], ssem.at[d + 2], rsem.at[d + 2], y_peer(d)))
    for c in copies:
        c.start()
    for c in copies:
        c.wait_recv()

    def total(own, got):
        t = own.astype(F32)
        for d in range(3):
            t = t + got[d].astype(F32)
        return t

    sa[...] = total(ga[x], ra).astype(BF)
    sb[...] = total(gb[y], rb).astype(BF)
    second = []
    for d in range(1, 4):
        second.append(remote(sa.at[(y + d) % 4], ra2.at[d - 1], ssem.at[d + 5], rsem.at[d + 5], y_peer(d)))
        second.append(remote(sb.at[(x + d) % 4], rb2.at[d - 1], ssem.at[d + 8], rsem.at[d + 8], x_peer(d)))
    for c in second:
        c.start()
    for c in second:
        c.wait_recv()
    pad = one_hot(64, 48, lambda o: jnp.where((o & 15) < 12, (o >> 4) * 12 + (o & 15), -1))
    tz[:, :, :768] = dot(pad, total(sa[y], ra2).astype(BF)).astype(BF).reshape(4, 16, 768)
    tz[:, :, 768:] = dot(pad, total(sb[x], rb2).astype(BF)).astype(BF).reshape(4, 16, 768)
    third = [
        remote(tz.at[(zh + d) % 4], rz.at[d - 1], ssem.at[d + 11], rsem.at[d + 11], z_peer(d)) for d in range(1, 4)
    ]
    for c in third:
        c.start()
    for c in third:
        c.wait_recv()
    tl[...] = total(tz[zh], rz).astype(BF)
    fourth = remote(tl, rl, ssem.at[15], rsem.at[15], across)
    fourth.start()
    pltpu.make_async_copy(brecv.at[pl.ds(0, 63)], brecv.at[pl.ds(0, 63)], brsem).wait()
    back = one_hot(192, 256, lambda o: (((o & 63) >> 2) << 4) + ((o >> 6) << 2) + (o & 3))
    for blk in range(4):
        rows = pl.ds(blk * 64, 64)
        got = dot(back, brecv[pl.ds(blk * 16, 16)].reshape(256, 256))
        for p in range(3):
            at = slice(p * 256, p * 256 + 256)
            gin_ref[rows, at] = (cot_ref[rows, at].astype(F32) + got[p * 64 : p * 64 + 64]).astype(BF)
    fourth.wait_recv()
    tc[...] = (tl[...].astype(F32) + rl[...].astype(F32)) * (1.0 / 256.0)
    fifth = remote(tc, rc, ssem.at[16], rsem.at[16], other)
    fifth.start()
    fifth.wait_recv()
    first = jnp.where(core == 0, tc[...], rc[...])
    last = jnp.where(core == 0, rc[...], tc[...])
    gqkv_ref[:, :1152] = first[:12, :1152]
    gqkv_ref[:, 1152:] = last[:12, :1152]
    gout_ref[:, :384] = first[:12, 1152:]
    gout_ref[:, 384:] = last[:12, 1152:]
    for c in copies + second + third + [fourth, fifth]:
        c.wait_send()
    pltpu.make_async_copy(bsend.at[pl.ds(0, 63)], bsend.at[pl.ds(0, 63)], bssem).wait()


VM = pl.BlockSpec(memory_space=pltpu.VMEM)


def params(cid=None, mib=40):
    if cid is None:
        return pltpu.CompilerParams(vmem_limit_bytes=mib << 20)
    return pltpu.CompilerParams(collective_id=cid, has_side_effects=True, vmem_limit_bytes=mib << 20)


def row_order():
    o = np.arange(768)
    yy, xx, zz, i = o // 192, (o // 48) % 4, (o // 12) % 4, o % 12
    m = np.zeros((768, 768), np.float32)
    m[o, yy * 192 + zz * 48 + xx * 12 + i] = 1.0
    return m


def local(activations, cotangent, qkv_weight, out_weight):
    act = activations.reshape(256, 768)
    cot = cotangent.reshape(256, 768)
    tokens = jax.ShapeDtypeStruct((256, 768), BF)
    xcol, ccol = pl.pallas_call(
        exchange_in,
        out_shape=(tokens, tokens),
        in_specs=[VM, VM],
        out_specs=(VM, VM),
        scratch_shapes=[
            pltpu.VMEM((64, 16, 384), BF),
            pltpu.VMEM((64, 16, 384), BF),
            pltpu.SemaphoreType.DMA,
            pltpu.SemaphoreType.DMA,
        ],
        compiler_params=params(0),
        name="exchange_in",
    )(act, cot)
    normed, gp, mixed, branch = pl.pallas_call(
        attend,
        out_shape=(tokens, jax.ShapeDtypeStruct((256, 2304), BF), tokens, tokens),
        in_specs=[VM] * 4,
        out_specs=(VM,) * 4,
        scratch_shapes=[pltpu.VMEM((256, 2304), BF), pltpu.VMEM((256, 768), BF)],
        compiler_params=params(),
        name="attend",
    )(xcol, ccol, qkv_weight, out_weight)
    order = jnp.asarray(row_order(), dtype=BF)
    gin, gqkv, gout = pl.pallas_call(
        reduce_out,
        out_shape=(tokens, jax.ShapeDtypeStruct((12, 2304), F32), jax.ShapeDtypeStruct((12, 768), F32)),
        in_specs=[VM] * 7,
        out_specs=(VM,) * 3,
        scratch_shapes=[
            pltpu.VMEM((512, 768), BF),
            pltpu.VMEM((512, 768), BF),
            pltpu.VMEM((512, 1152), BF),
            pltpu.VMEM((512, 384), BF),
            pltpu.VMEM((64, 16, 256), BF),
            pltpu.VMEM((64, 16, 256), BF),
            pltpu.VMEM((4, 4, 48, 768), BF),
            pltpu.VMEM((4, 4, 48, 768), BF),
            pltpu.VMEM((3, 4, 48, 768), BF),
            pltpu.VMEM((3, 4, 48, 768), BF),
            pltpu.VMEM((4, 48, 768), BF),
            pltpu.VMEM((4, 48, 768), BF),
            pltpu.VMEM((3, 48, 768), BF),
            pltpu.VMEM((3, 48, 768), BF),
            pltpu.VMEM((4, 16, 1536), BF),
            pltpu.VMEM((3, 16, 1536), BF),
            pltpu.VMEM((16, 1536), BF),
            pltpu.VMEM((16, 1536), BF),
            pltpu.VMEM((16, 1536), F32),
            pltpu.VMEM((16, 1536), F32),
            pltpu.SemaphoreType.DMA((4,)),
            pltpu.SemaphoreType.DMA((4,)),
            pltpu.SemaphoreType.DMA,
            pltpu.SemaphoreType.DMA,
            pltpu.SemaphoreType.DMA((17,)),
            pltpu.SemaphoreType.DMA((17,)),
        ],
        compiler_params=params(1),
        name="reduce_out",
    )(normed, gp, mixed, ccol, branch, cot, order)
    return gin.reshape(activations.shape), gqkv, gout


def solution(mesh):
    return jax.shard_map(
        local,
        mesh=mesh,
        in_specs=(P("batch", "band", None, None), P("batch", "band", None, None), P(), P()),
        out_specs=(P("batch", "band", None, None), P("band", None), P("band", None)),
        check_vma=False,
    )
```

time: 695 us -> 102 us (0.15)
  blocking collectives: 305 us -> 0 us
  starting transfers between devices: 124 us -> 0 us
  local copies, waits for them, and re-layouts: 116 us -> 7.29 us
  Pallas kernels: 0 us -> 93.3 us
  waiting for transfers between devices: 69.6 us -> 0 us
  matrix products: 37.7 us -> 0 us
  other arithmetic: 22.4 us -> 0 us
  between operations: 15.1 us -> 0.69 us
    unnamed x1 -> x0, blocking collectives: 305 us -> none
    unnamed x32 -> x0, starting transfers between devices: 96.2 us -> none
    pallas_call x0 -> x3, Pallas kernels: none -> 93.3 us  [the longest x1 54.3 us: local(): pl.pallas_call(reduce_out, out_shape=(tokens, jax.ShapeDtypeStruct((12, 2...]
    unnamed x66 -> x15, local copies, waits for them, and re-layouts: 72.7 us -> 7.29 us
    psum x1 -> x0, waiting for transfers between devices: 57.4 us -> none  [local(): lax.psum(qkv_rows.astype(jnp.bfloat16), 'batch').astype(jnp.float32)]
    dot_general x10 -> x0, matrix products: 32.9 us -> none  [the longest x1 5.23 us: local(): jnp.einsum('bcnij,bicnh->bjcnh', grad_score, queries, preferred_element_t...]
    all_to_all x3 -> x0, starting transfers between devices: 28 us -> none  [the longest x1 15.3 us: local(): lax.all_to_all(activations, 'band', split_axis=2, concat_axis=1, tiled=True)]
    convert_element_type x8 -> x0, local copies, waits for them, and re-layouts: 22 us -> none  [the longest x2 9.97 us: local(): grad_proj = jnp.stack([grad_query, grad_key, grad_value], axis=3).astype(...]
  transfers between devices with their start and end apart: 36 -> 0, of which waited for: 3 -> 0; matrix products, arithmetic and copies ran while one was open for 56% -> 0% of each run, Pallas kernels for 0% -> 0%
where the time goes in v1:
time: 102 us; the launch traced here: 101 us
  Pallas kernels  93.3 us (91%)
  local copies, waits for them, and re-layouts  7.29 us (7%)
    pallas_call x1, Pallas kernels, local(): pl.pallas_call(reduce_out, out_shape=(tokens, jax.ShapeDtypeStruct((12, 2...  54.3 us
    pallas_call x1, Pallas kernels, local(): pl.pallas_call(exchange_in, out_shape=(tokens, tokens), in_specs=[VM, VM]...  29.3 us
    pallas_call x1, Pallas kernels, local(): pl.pallas_call(attend, out_shape=(tokens, jax.ShapeDtypeStruct((256, 2304...  9.7 us
    unnamed x15, local copies, waits for them, and re-layouts  7.29 us

profile of v1, /device:TPU:1, one launch (start us, length us, event | category | flops | bytes accessed | tf_op | source)
XLA Modules:
  0.0 101.3 jit_solution(10865889391905336501)
XLA Ops:
  0.6 0.0 copy-start.1
  0.6 1.0 copy-done.1
  1.6 0.0 copy-start.5
  1.6 1.0 copy-done.5
  2.6 29.3 %exchange_in.1 = (bf16[256,768]{1,0:T(8,128)(2,1)S(1)}, bf16[256,768]{1,0:T(8,128)(2,1)S(1)}) custom-call(bf16[256,768]{1,0:T(8,128)(2,1)S(1)} %bitcast.5, bf16[256,768]{1,0:T(8,128)(2,1)S(1)} %bitcast.3), custom_call_target="tpu_custom_call" | custom-call | tf_op jit(solution)/shard_map/exchange_in/pallas_call | solution.py:295
  31.9 0.0 copy-start
  32.0 2.0 %copy-done = bf16[768,2304]{1,0:T(8,128)(2,1)S(1)} copy-done((bf16[768,2304]{1,0:T(8,128)(2,1)S(1)}, bf16[768,2304]{1,0:T(8,128)(2,1)}, u32[]{:S(2)}) %copy-start) | copy-done | bytes 3538968
  34.0 0.0 copy-start.3
  34.0 1.3 %copy-done.3 = bf16[768,768]{1,0:T(8,128)(2,1)S(1)} copy-done((bf16[768,768]{1,0:T(8,128)(2,1)S(1)}, bf16[768,768]{1,0:T(8,128)(2,1)}, u32[]{:S(2)}) %copy-start.3) | copy-done | bytes 1179672
  35.2 0.0 copy-start.2
  35.2 0.0 copy-start.4
  35.2 9.7 %attend.1 = (bf16[256,768]{1,0:T(8,128)(2,1)S(1)}, bf16[256,2304]{1,0:T(8,128)(2,1)S(1)}, bf16[256,768]{1,0:T(8,128)(2,1)S(1)}, bf16[256,768]{1,0:T(8,128)(2,1)S(1)}) custom-call(bf16[256,768]{1,0:T(8,128)(2,1)S(1)} %get-tuple-element.12.x_ref, bf16[256,768]{1,0:T(8,128)(2,1)S(1)} %get-tuple-element.13.c_ref.ccol_ref, bf16[768,2304]{1,0:T(8,128)(2,1)S(1)} %copy-done, ...), custom_call_target="tpu_custom_call" | custom-call | tf_op jit(solution)/shard_map/attend/pallas_call | solution.py:309
  44.9 0.0 copy-done.2
  44.9 0.0 copy-done.4
  45.0 54.3 %reduce_out.1 = (bf16[256,768]{1,0:T(8,128)(2,1)S(1)}, f32[12,2304]{1,0:T(8,128)S(1)}, f32[12,768]{1,0:T(8,128)S(1)}) custom-call(bf16[256,768]{1,0:T(8,128)(2,1)S(1)} %get-tuple-element.14.normed_ref, bf16[256,2304]{1,0:T(8,128)(2,1)S(1)} %get-tuple-element.15.gp_ref, bf16[256,768]{1,0:T(8,128)(2,1)S(1)} %get-tuple-element.16.mixed_ref, ...), custom_call_target="tpu_custom_call" | custom-call | tf_op jit(solution)/shard_map/reduce_out/pallas_call | solution.py:319
  99.2 0.7 copy.11
  100.0 0.7 copy.12
  100.7 0.6 copy.13
Async XLA Ops:
  0.6 1.0 copy-start.1
  1.6 1.0 copy-start.5
  31.9 2.0 %copy-start = (bf16[768,2304]{1,0:T(8,128)(2,1)S(1)}, bf16[768,2304]{1,0:T(8,128)(2,1)}, u32[]{:S(2)}) copy-start(bf16[768,2304]{1,0:T(8,128)(2,1)} %wqkv_ref.1) | copy-start | bytes 10616836
  34.0 1.3 %copy-start.3 = (bf16[768,768]{1,0:T(8,128)(2,1)S(1)}, bf16[768,768]{1,0:T(8,128)(2,1)}, u32[]{:S(2)}) copy-start(bf16[768,768]{1,0:T(8,128)(2,1)} %wout_ref.1) | copy-start | bytes 3538948
  35.2 9.7 %copy-start.2 = (bf16[1,1,256,768]{3,2,1,0:T(8,128)(2,1)S(1)}, bf16[1,1,256,768]{3,2,1,0:T(8,128)(2,1)}, u32[]{:S(2)}) copy-start(bf16[1,1,256,768]{3,2,1,0:T(8,128)(2,1)} %param.6) | copy-start | bytes 1179652
  35.2 9.7 %copy-start.4 = (bf16[768,768]{1,0:T(8,128)(2,1)S(1)}, bf16[768,768]{1,0:T(8,128)(2,1)}, u32[]{:S(2)}) copy-start(bf16[768,768]{1,0:T(8,128)(2,1)} %constant.2.clone.order_ref) | copy-start | bytes 3538948

commit v2 on v0

v2 whole, which is shorter than its diff:
```python
import functools

import jax
import jax.numpy as jnp
import numpy as np
from jax import lax
from jax.experimental import pallas as pl
from jax.experimental.pallas import tpu as pltpu
from jax.sharding import PartitionSpec as P

HEADS = 12
HD = 64
EPSILON = 1e-06
MESH = pl.DeviceIdType.MESH
BF = jnp.bfloat16
F32 = jnp.float32
GROUP = 4
WIDE = GROUP * HD
PAIRS = HEADS // GROUP
BATCH = 6


def one_hot(rows, cols, index):
    o = lax.broadcasted_iota(jnp.int32, (rows, cols), 0)
    i = lax.broadcasted_iota(jnp.int32, (rows, cols), 1)
    return jnp.where(index(o) == i, 1.0, 0.0).astype(BF)


def dot(a, b, ca=1, cb=0):
    return lax.dot_general(a, b, (((ca,), (cb,)), ((), ())), preferred_element_type=F32)


def remote(src, dst, s, r, to):
    return pltpu.make_async_remote_copy(
        src_ref=src, dst_ref=dst, send_sem=s, recv_sem=r, device_id=to, device_id_type=MESH
    )


def body(
    act_hbm, cot_hbm, wqkv_hbm, wout_hbm, ordx_hbm, ordy_hbm,
    gin_hbm, gqkv_hbm, gout_hbm,
    gin_ref, gqkv_ref, gout_ref, out_sem,
    act, cot, wqkv, wout, ordx, ordy,
    send, recv, bsend, brecv,
    x_ref, c_ref, normed, proj, gm, gp, mixed, prob,
    nfx, nfy, mfx, cfull, gfull,
    grad, ring, summed, second, padded, zin, fin,
    load_sem, a2a_s, a2a_r, fac_s, fac_r, ring_s, ring_r, sec_s, sec_r, z_s, z_r, fin_s, fin_r,
):
    band = lax.axis_index("band")
    batch = lax.axis_index("batch")
    y, zh, x = band // 16, (band // 4) % 4, band % 4
    zl, core = batch // 2, batch % 2
    z = zh * 2 + zl

    def peer_of(k):
        return ((y + k // 16) % 4) * 16 + ((zh + (k // 4) % 4) % 4) * 4 + (x + k % 4) % 4

    def at_x(d):
        return (y * 16 + zh * 4 + (x + d) % 4, batch)

    def at_y(d):
        return (((y + d) % 4) * 16 + zh * 4 + x, batch)

    def at_z(d):
        t = (z + d) % 8
        return (y * 16 + (t // 2) * 4 + x, (t % 2) * 2 + core)

    other = (band, zl * 2 + 1 - core)
    across = (band, (1 - zl) * 2 + core)
    corner = (band, (1 - zl) * 2 + 1 - core)

    loads = [
        pltpu.make_async_copy(src, dst, load_sem.at[i])
        for i, (src, dst) in enumerate(
            [(act_hbm, act), (cot_hbm, cot), (wqkv_hbm, wqkv), (ordx_hbm, ordx), (ordy_hbm, ordy), (wout_hbm, wout)]
        )
    ]
    for c in loads:
        c.start()
    barrier = pltpu.get_barrier_semaphore()

    def greet(k, _):
        pl.semaphore_signal(barrier, 1, device_id=(peer_of(k), batch), device_id_type=MESH)
        return 0

    lax.fori_loop(1, 64, greet, 0)
    pl.semaphore_signal(barrier, 1, device_id=other, device_id_type=MESH)
    pl.semaphore_signal(barrier, 1, device_id=corner, device_id_type=MESH)
    for d in (1, 3, 5, 7):
        pl.semaphore_signal(barrier, 1, device_id=at_z(d), device_id_type=MESH)

    fill = one_hot(128, 128, lambda o: ((o >> 2) & 1) * 64 + (o >> 3) * 4 + (o & 3))

    def pack(src, slot):
        for g in range(4):
            rows = pl.ds(g * 64, 64)
            stack = jnp.concatenate([src[rows, :384], src[rows, 384:]], axis=0)
            send[slot, pl.ds(g * 16, 16)] = dot(fill, stack).astype(BF).reshape(16, 8, 384)

    def push(group, src, dst, s, r):
        def one(dz, k):
            peer = ((y + k // 4) % 4) * 16 + ((zh + dz) % 4) * 4 + (x + k % 4) % 4
            pltpu.make_async_remote_copy(
                src_ref=src.at[peer],
                dst_ref=dst.at[band],
                send_sem=s.at[group],
                recv_sem=r.at[group],
                device_id=(peer, batch),
                device_id_type=MESH,
            ).start()

        def far(k, _):
            one(2, k)
            return 0

        def near(k, _):
            one(1, k)
            one(3, k)
            return 0

        def plane(k, _):
            one(0, k)
            return 0

        if group == 0:
            lax.fori_loop(0, 16, far, 0)
        elif group == 1:
            lax.fori_loop(0, 16, near, 0)
        else:
            lax.fori_loop(1, 16, plane, 0)
            dst[band] = src[band]

    def arrive(group, dst, sem):
        n = (16, 32, 15)[group]
        pltpu.make_async_copy(dst.at[pl.ds(0, n)], dst.at[pl.ds(0, n)], sem.at[group]).wait()

    loads[0].wait()
    pack(act, 0)
    pl.semaphore_wait(barrier, 69)
    for g in range(3):
        push(g, send.at[0], recv.at[0], a2a_s.at[0], a2a_r.at[0])
    loads[1].wait()
    pack(cot, 1)
    arrive(0, recv.at[0], a2a_r.at[0])
    for g in range(3):
        push(g, send.at[1], recv.at[1], a2a_s.at[1], a2a_r.at[1])

    empty = one_hot(128, 128, lambda o: ((o & 15) << 3) + ((o >> 6) << 2) + ((o >> 4) & 3))

    def unpack(slot, dst):
        for blk in range(4):
            got = recv[slot, pl.ds(blk * 16, 16)].reshape(128, 384)
            out = dot(empty, got).astype(BF)
            for t in range(4):
                rows = pl.ds(t * 64 + blk * 16, 16)
                dst[rows, :384] = out[t * 16 : t * 16 + 16]
                dst[rows, 384:] = out[64 + t * 16 : 64 + t * 16 + 16]

    arrive(2, recv.at[0], a2a_r.at[0])
    arrive(1, recv.at[0], a2a_r.at[0])
    unpack(0, x_ref)
    as_float = x_ref[...].astype(F32)
    inverse = lax.rsqrt(jnp.mean(as_float * as_float, axis=-1, keepdims=True) + EPSILON)
    normed[...] = (as_float * inverse).astype(BF)
    loads[2].wait()
    proj[...] = dot(normed[...], wqkv[...]).astype(BF)
    half = pl.ds(pl.multiple_of(core * 256, 256), 256)
    loads[3].wait()
    loads[4].wait()
    nfx[:, half] = dot(ordx[...], normed[...], 1, 1).astype(BF)
    nfy[:, half] = dot(ordy[...], normed[...], 1, 1).astype(BF)
    fx = remote(nfx.at[:, half], nfx.at[:, half], fac_s.at[0], fac_r.at[0], other)
    fy = remote(nfy.at[:, half], nfy.at[:, half], fac_s.at[1], fac_r.at[1], other)
    fx.start()
    fy.start()

    scale = HD ** (-0.5)
    lane = lax.broadcasted_iota(jnp.int32, (1, WIDE), 1) // HD
    masks = [lane == g for g in range(GROUP)]

    def spread(v):
        zero = jnp.zeros_like(v)
        return jnp.concatenate([jnp.where(m, v, zero) for m in masks], axis=0)

    def gather(r):
        out = r[0:64]
        for g in range(1, GROUP):
            out = jnp.where(masks[g], r[g * 64 : g * 64 + 64], out)
        return out

    each = [(c, h) for c in range(4) for h in range(PAIRS)]
    batches = [each[n : n + BATCH] for n in range(0, len(each), BATCH)]

    def take(ref, off, it):
        return [ref[pl.ds(c * 64, 64), off + h * WIDE : off + h * WIDE + WIDE] for c, h in it]

    def put(ref, it, values):
        for (c, h), v in zip(it, values):
            ref[pl.ds(c * 64, 64), h * WIDE : h * WIDE + WIDE] = v

    for it in batches:
        qs = [spread(t) for t in take(proj, 0, it)]
        s = [dot(k, q, 1, 1) * scale for k, q in zip(take(proj, 768, it), qs)]
        e = [jnp.exp(t - jnp.max(t, axis=0, keepdims=True)) for t in s]
        p = [t * (1.0 / jnp.sum(t, axis=0, keepdims=True)) for t in e]
        for (c, h), t in zip(it, p):
            prob[c * PAIRS + h] = t
        put(mixed, it, [gather(dot(t.astype(BF), v, 0, 0)).astype(BF) for t, v in zip(p, take(proj, 1536, it))])
    mfx[:, half] = dot(ordx[...], mixed[...], 1, 1).astype(BF)
    fm = remote(mfx.at[:, half], mfx.at[:, half], fac_s.at[2], fac_r.at[2], other)
    fm.start()

    own_c = pl.ds(pl.multiple_of(core * 384, 128), 384)
    their_c = pl.ds(pl.multiple_of((1 - core) * 384, 128), 384)
    loads[5].wait()
    for g in range(3):
        arrive(g, recv.at[1], a2a_r.at[1])
    unpack(1, c_ref)
    fc = remote(c_ref.at[:, their_c], cfull.at[half], fac_s.at[3], fac_r.at[3], other)
    fc.start()
    cfull[half] = c_ref[:, own_c]
    gm[...] = dot(c_ref[...], wout[...], 1, 1).astype(BF)
    for it in batches:
        gs = [spread(t) for t in take(gm, 0, it)]
        p = [prob[c * PAIRS + h].astype(BF) for c, h in it]
        put(gp.at[2], it, [dot(a, b).astype(BF) for a, b in zip(p, gs)])

    def share(s):
        cp = remote(gp.at[s, :, their_c], gfull.at[s, half], fac_s.at[4 + s], fac_r.at[4 + s], other)
        cp.start()
        gfull[s, half] = gp[s, :, own_c]
        return cp

    fv = share(2)

    def first_axis(m):
        return (x, at_x) if m % 2 == 0 else (y, at_y)

    def second_axis(m):
        return (y, at_y) if m % 2 == 0 else (x, at_x)

    def block(pos, part):
        return pl.ds(pl.multiple_of((pos % 4) * 192 + part * 96, 96), 96)

    def ring_copy(m, i, src, to):
        return remote(src, ring.at[m, i], ring_s.at[m, i], ring_r.at[m, i], to)

    def ring_start(m):
        pos, to = first_axis(m)
        g = grad.at[m]
        cps = [
            ring_copy(m, 0, g.at[block(pos + 2, 0)], to(1)),
            ring_copy(m, 1, g.at[block(pos + 2, 1)], to(3)),
            ring_copy(m, 2, g.at[block(pos + 3, 0)], to(3)),
            ring_copy(m, 3, g.at[block(pos + 1, 1)], to(1)),
        ]
        for c in cps:
            c.start()
        return cps

    def ring_pass(m, cps):
        pos, to = first_axis(m)
        cps[0].wait_recv()
        b = block(pos + 1, 0)
        grad[m, b] = (grad[m, b].astype(F32) + ring[m, 0].astype(F32)).astype(BF)
        cps.append(ring_copy(m, 4, grad.at[m, b], to(1)))
        cps[4].start()
        cps[1].wait_recv()
        b = block(pos + 3, 1)
        grad[m, b] = (grad[m, b].astype(F32) + ring[m, 1].astype(F32)).astype(BF)
        cps.append(ring_copy(m, 5, grad.at[m, b], to(3)))
        cps[5].start()

    def ring_end(m, cps):
        pos, _ = first_axis(m)
        for c in cps[2:]:
            c.wait_recv()
        for part, i, j in ((0, 2, 4), (1, 3, 5)):
            t = grad[m, block(pos, part)].astype(F32) + ring[m, i].astype(F32) + ring[m, j].astype(F32)
            summed[m, pl.ds(part * 96, 96)] = t.astype(BF)

    def row48(pos):
        return pl.ds(pl.multiple_of((pos % 4) * 48, 48), 48)

    def second_start(m):
        pos, to = second_axis(m)
        cps = [
            remote(summed.at[m, row48(pos + d)], second.at[m, d - 1], sec_s.at[m, d - 1], sec_r.at[m, d - 1], to(d))
            for d in (2, 1, 3)
        ]
        for c in cps:
            c.start()
        return cps

    pad = one_hot(64, 48, lambda o: jnp.where((o & 15) < 12, (o >> 4) * 12 + (o & 15), -1))

    def second_end(m, cps):
        pos, _ = second_axis(m)
        for c in cps:
            c.wait_recv()
        t = summed[m, row48(pos)].astype(F32)
        for d in range(3):
            t = t + second[m, d].astype(F32)
        padded[m] = dot(pad, t.astype(BF)).astype(BF).reshape(4, 16, 384)

    def z_start(pair):
        out = []
        for d in (4, 3, 5, 2, 6, 1, 7):
            to = (z + d) % 8
            cp = remote(
                padded.at[pair * 2 + to % 2, to // 2], zin.at[pair, z], z_s.at[pair, d - 1], z_r.at[pair, d - 1], at_z(d)
            )
            cp.start()
            out.append(cp)
        zin[pair, z] = padded[pair * 2 + zl, zh]
        return out

    def z_end(pair, cps):
        for c in cps:
            c.wait_recv()
        t = zin[pair, 0].astype(F32)
        for i in range(1, 8):
            t = t + zin[pair, i].astype(F32)
        fin[pair, batch] = (t * (1.0 / 256.0)).astype(BF)
        out = []
        for i, to in enumerate((other, across, corner)):
            cp = remote(fin.at[pair, batch], fin.at[pair, batch], fin_s.at[pair, i], fin_r.at[pair, i], to)
            cp.start()
            out.append(cp)
        return out

    fm.wait_recv()
    fc.wait_recv()
    grad[0] = dot(mfx[...], cfull[...]).astype(BF)
    r0 = ring_start(0)
    fy.wait_recv()
    fv.wait_recv()
    grad[1] = dot(nfy[...], gfull[2]).astype(BF)
    r1 = ring_start(1)
    for it in batches:
        gs = [spread(t) for t in take(gm, 0, it)]
        dp = [dot(v, g, 1, 1) for v, g in zip(take(proj, 1536, it), gs)]
        p = [prob[c * PAIRS + h] for c, h in it]
        ds = [(a * (d - jnp.sum(a * d, axis=0, keepdims=True)) * scale).astype(BF) for a, d in zip(p, dp)]
        put(gp.at[0], it, [gather(dot(d, k, 0, 0)).astype(BF) for d, k in zip(ds, take(proj, 768, it))])
        qs = [spread(t) for t in take(proj, 0, it)]
        put(gp.at[1], it, [dot(d, q).astype(BF) for d, q in zip(ds, qs)])
    fq = share(0)
    fk = share(1)
    ring_pass(0, r0)
    ring_pass(1, r1)
    fx.wait_recv()
    fq.wait_recv()
    grad[2] = dot(nfx[...], gfull[0]).astype(BF)
    r2 = ring_start(2)
    fk.wait_recv()
    grad[3] = dot(nfy[...], gfull[1]).astype(BF)
    r3 = ring_start(3)
    gn = dot(gp[0], wqkv[:, :768], 1, 1) + dot(gp[1], wqkv[:, 768:1536], 1, 1) + dot(gp[2], wqkv[:, 1536:], 1, 1)
    xf = x_ref[...].astype(F32)
    centre = jnp.mean(gn * xf, axis=-1, keepdims=True)
    branch = (inverse * gn - xf * (inverse * inverse * inverse * centre)).astype(BF)
    back = one_hot(128, 128, lambda o: ((o >> 2) & 1) * 64 + (o & 3) * 16 + (o >> 3))
    for blk in range(4):
        stack = jnp.concatenate(
            [branch[t * 64 + blk * 16 : t * 64 + blk * 16 + 16, p * 384 : p * 384 + 384] for p in range(2) for t in range(4)],
            axis=0,
        )
        bsend[pl.ds(blk * 16, 16)] = dot(back, stack).astype(BF).reshape(16, 8, 384)
    ring_pass(2, r2)
    ring_pass(3, r3)
    for g in range(3):
        push(g, bsend, brecv, a2a_s.at[2], a2a_r.at[2])
    ring_end(0, r0)
    s0 = second_start(0)
    ring_end(1, r1)
    s1 = second_start(1)
    ring_end(2, r2)
    s2 = second_start(2)
    ring_end(3, r3)
    s3 = second_start(3)
    second_end(0, s0)
    second_end(1, s1)
    z0 = z_start(0)
    second_end(2, s2)
    second_end(3, s3)
    z1 = z_start(1)
    e0 = z_end(0, z0)
    for g in range(3):
        arrive(g, brecv, a2a_r.at[2])
    home = one_hot(128, 128, lambda o: (((o & 63) >> 2) << 3) + ((o >> 6) << 2) + (o & 3))
    for blk in range(4):
        rows = pl.ds(blk * 64, 64)
        got = dot(home, brecv[pl.ds(blk * 16, 16)].reshape(128, 384))
        gin_ref[rows, :384] = (cot[rows, :384].astype(F32) + got[:64]).astype(BF)
        gin_ref[rows, 384:] = (cot[rows, 384:].astype(F32) + got[64:]).astype(BF)
    outs = [
        pltpu.make_async_copy(src, dst, out_sem.at[i])
        for i, (src, dst) in enumerate([(gin_ref, gin_hbm), (gqkv_ref, gqkv_hbm), (gout_ref, gout_hbm)])
    ]
    outs[0].start()
    e1 = z_end(1, z1)
    for pair, cps in ((0, e0), (1, e1)):
        for c in cps:
            c.wait_recv()
        for q in range(4):
            m = pair * 2 + q // 2
            at = (0, 1536, 0, 768)[m] + (q % 2) * 384
            dst = gout_ref if m == 0 else gqkv_ref
            dst[:, at : at + 384] = fin[pair, q].astype(F32)[:12]
    outs[1].start()
    outs[2].start()
    for c in [fx, fy, fm, fc, fv, fq, fk] + r0 + r1 + r2 + r3 + s0 + s1 + s2 + s3 + z0 + z1 + e0 + e1:
        c.wait_send()
    for g in range(3):
        arrive(g, send.at[0], a2a_s.at[0])
        arrive(g, send.at[1], a2a_s.at[1])
        arrive(g, bsend, a2a_s.at[2])
    for c in outs:
        c.wait()


def hand_over(a, b, c, a_out, b_out, c_out, va, vb, vc, sem):
    here = [pltpu.make_async_copy(src, dst, sem.at[i]) for i, (src, dst) in enumerate([(a, va), (b, vb), (c, vc)])]
    away = [
        pltpu.make_async_copy(src, dst, sem.at[i + 3]) for i, (src, dst) in enumerate([(va, a_out), (vb, b_out), (vc, c_out)])
    ]
    for cp in here:
        cp.start()
    for first, then in zip(here, away):
        first.wait()
        then.start()
    for cp in away:
        cp.wait()


def orders():
    o = np.arange(768)
    a, b, c, i = o // 192, (o // 48) % 4, (o // 12) % 4, o % 12
    out = []
    for yy, xx in ((b, a), (a, b)):
        m = np.zeros((768, 768), np.float32)
        m[o, yy * 192 + c * 48 + xx * 12 + i] = 1.0
        out.append(jnp.asarray(m, dtype=BF))
    return out


def local(activations, cotangent, qkv_weight, out_weight):
    act = activations.reshape(256, 768)
    cot = cotangent.reshape(256, 768)
    ordx, ordy = orders()
    vm = pltpu.VMEM
    dma = pltpu.SemaphoreType.DMA
    hbm = pl.BlockSpec(memory_space=pltpu.HBM)
    gin, gqkv, gout = pl.pallas_call(
        body,
        out_shape=(
            jax.ShapeDtypeStruct((256, 768), BF),
            jax.ShapeDtypeStruct((12, 2304), F32),
            jax.ShapeDtypeStruct((12, 768), F32),
        ),
        in_specs=[hbm] * 6,
        out_specs=(hbm,) * 3,
        scratch_shapes=[
            vm((256, 768), BF),
            vm((12, 2304), F32),
            vm((12, 768), F32),
            dma((3,)),
            vm((256, 768), BF),
            vm((256, 768), BF),
            vm((768, 2304), BF),
            vm((768, 768), BF),
            vm((768, 768), BF),
            vm((768, 768), BF),
            vm((2, 64, 8, 384), BF),
            vm((2, 64, 8, 384), BF),
            vm((64, 8, 384), BF),
            vm((64, 8, 384), BF),
            vm((256, 768), BF),
            vm((256, 768), BF),
            vm((256, 768), BF),
            vm((256, 2304), BF),
            vm((256, 768), BF),
            vm((3, 256, 768), BF),
            vm((256, 768), BF),
            vm((4 * PAIRS, 64, WIDE), F32),
            vm((768, 512), BF),
            vm((768, 512), BF),
            vm((768, 512), BF),
            vm((512, 384), BF),
            vm((3, 512, 384), BF),
            vm((4, 768, 384), BF),
            vm((4, 6, 96, 384), BF),
            vm((4, 192, 384), BF),
            vm((4, 3, 48, 384), BF),
            vm((4, 4, 16, 384), BF),
            vm((2, 8, 16, 384), BF),
            vm((2, 4, 16, 384), BF),
            dma((6,)),
            dma((3, 3)),
            dma((3, 3)),
            dma((7,)),
            dma((7,)),
            dma((4, 6)),
            dma((4, 6)),
            dma((4, 3)),
            dma((4, 3)),
            dma((2, 7)),
            dma((2, 7)),
            dma((2, 3)),
            dma((2, 3)),
        ],
        compiler_params=pltpu.CompilerParams(collective_id=0, has_side_effects=True, vmem_limit_bytes=62 << 20),
        name="column_backward",
    )(act, cot, qkv_weight, out_weight, ordx, ordy)
    gin, gqkv, gout = pl.pallas_call(
        hand_over,
        out_shape=tuple(jax.ShapeDtypeStruct(v.shape, v.dtype) for v in (gin, gqkv, gout)),
        in_specs=[hbm] * 3,
        out_specs=(hbm,) * 3,
        scratch_shapes=[vm((256, 768), BF), vm((12, 2304), F32), vm((12, 768), F32), dma((6,))],
        name="hand_over",
    )(gin, gqkv, gout)
    return gin.reshape(activations.shape), gqkv, gout


def solution(mesh):
    return jax.shard_map(
        local,
        mesh=mesh,
        in_specs=(P("batch", "band", None, None), P("batch", "band", None, None), P(), P()),
        out_specs=(P("batch", "band", None, None), P("band", None), P("band", None)),
        check_vma=False,
    )
```

time: 695 us -> 74.1 us (0.11)
  blocking collectives: 305 us -> 0 us
  starting transfers between devices: 124 us -> 0 us
  local copies, waits for them, and re-layouts: 116 us -> 0 us
  Pallas kernels: 0 us -> 73.4 us
  waiting for transfers between devices: 69.6 us -> 0 us
  matrix products: 37.7 us -> 0 us
  other arithmetic: 22.4 us -> 0 us
  between operations: 15.1 us -> 0.64 us
    unnamed x1 -> x0, blocking collectives: 305 us -> none
    unnamed x32 -> x0, starting transfers between devices: 96.2 us -> none
    pallas_call x0 -> x2, Pallas kernels: none -> 73.4 us  [the longest x1 71.5 us: local(): pl.pallas_call(body, out_shape=(jax.ShapeDtypeStruct((256, 768), BF), jax...]
    unnamed x66 -> x0, local copies, waits for them, and re-layouts: 72.7 us -> none
    psum x1 -> x0, waiting for transfers between devices: 57.4 us -> none  [local(): lax.psum(qkv_rows.astype(jnp.bfloat16), 'batch').astype(jnp.float32)]
    dot_general x10 -> x0, matrix products: 32.9 us -> none  [the longest x1 5.23 us: local(): jnp.einsum('bcnij,bicnh->bjcnh', grad_score, queries, preferred_element_t...]
    all_to_all x3 -> x0, starting transfers between devices: 28 us -> none  [the longest x1 15.3 us: local(): lax.all_to_all(activations, 'band', split_axis=2, concat_axis=1, tiled=True)]
    convert_element_type x8 -> x0, local copies, waits for them, and re-layouts: 22 us -> none  [the longest x2 9.97 us: local(): grad_proj = jnp.stack([grad_query, grad_key, grad_value], axis=3).astype(...]
  transfers between devices with their start and end apart: 36 -> 0, of which waited for: 3 -> 0; matrix products, arithmetic and copies ran while one was open for 56% -> 0% of each run, Pallas kernels for 0% -> 0%
where the time goes in v2:
time: 74.1 us; the launch traced here: 74 us
  Pallas kernels  73.4 us (99%)
    pallas_call x1, Pallas kernels, local(): pl.pallas_call(body, out_shape=(jax.ShapeDtypeStruct((256, 768), BF), jax...  71.5 us
    pallas_call x1, Pallas kernels, local(): pl.pallas_call(hand_over, out_shape=tuple((jax.ShapeDtypeStruct(v.shape,...  1.85 us

profile of v2, /device:TPU:1, one launch (start us, length us, event | category | flops | bytes accessed | tf_op | source)
XLA Modules:
  0.0 74.0 jit_solution(3524179544961336076)
XLA Ops:
  0.6 71.5 %column_backward.1 = (bf16[256,768]{1,0:T(8,128)(2,1)}, f32[12,2304]{1,0:T(8,128)}, f32[12,768]{1,0:T(8,128)}) custom-call(bf16[256,768]{1,0:T(8,128)(2,1)} %bitcast.3, bf16[256,768]{1,0:T(8,128)(2,1)} %bitcast.4, bf16[768,2304]{1,0:T(8,128)(2,1)} %wqkv_hbm.1, bf16[768,768]{1,0:T(8,128)(2,1)} %wout_hbm.1, bf16[768,768]{1,0:T(8,128)(2,1)} %constant.4.clone.ordx_hbm, ...), custom_call_target="tpu_custom_call" | custom-call | tf_op jit(solution)/shard_map/column_backward/pallas_call | solution.py:456
  72.1 1.8 %hand_over.1 = (bf16[256,768]{1,0:T(8,128)(2,1)}, f32[12,2304]{1,0:T(8,128)}, f32[12,768]{1,0:T(8,128)}) custom-call(bf16[256,768]{1,0:T(8,128)(2,1)} %get-tuple-element.9.a, f32[12,2304]{1,0:T(8,128)} %get-tuple-element.10.b, f32[12,768]{1,0:T(8,128)} %get-tuple-element.11.c), custom_call_target="tpu_custom_call" | custom-call | tf_op jit(solution)/shard_map/hand_over/pallas_call | solution.py:517

commit v3 on v2

--- a/solution.py
+++ b/solution.py
@@ -17,6 +17,7 @@
 GROUP = 4
 WIDE = GROUP * HD
 PAIRS = HEADS // GROUP
+DIRECT = ()
 BATCH = 6
 
 
@@ -45,7 +46,7 @@
     x_ref, c_ref, normed, proj, gm, gp, mixed, prob,
     nfx, nfy, mfx, cfull, gfull,
     grad, ring, summed, second, padded, zin, fin,
-    load_sem, a2a_s, a2a_r, fac_s, fac_r, ring_s, ring_r, sec_s, sec_r, z_s, z_r, fin_s, fin_r,
+    plane_in, load_sem, a2a_s, a2a_r, fac_s, fac_r, ring_s, ring_r, sec_s, sec_r, z_s, z_r, fin_s, fin_r,
 ):
     band = lax.axis_index("band")
     batch = lax.axis_index("batch")
@@ -53,9 +54,6 @@
     zl, core = batch // 2, batch % 2
     z = zh * 2 + zl
 
-    def peer_of(k):
-        return ((y + k // 16) % 4) * 16 + ((zh + (k // 4) % 4) % 4) * 4 + (x + k % 4) % 4
-
     def at_x(d):
         return (y * 16 + zh * 4 + (x + d) % 4, batch)
 
@@ -76,19 +74,17 @@
             [(act_hbm, act), (cot_hbm, cot), (wqkv_hbm, wqkv), (ordx_hbm, ordx), (ordy_hbm, ordy), (wout_hbm, wout)]
         )
     ]
-    for c in loads:
+    loads[0].start()
+    barrier = pltpu.get_barrier_semaphore()
+    for k in range(1, 16):
+        to = ((y + k // 4) % 4) * 16 + zh * 4 + (x + k % 4) % 4
+        pl.semaphore_signal(barrier, 1, device_id=(to, batch), device_id_type=MESH)
+    for d in range(1, 8):
+        pl.semaphore_signal(barrier, 1, device_id=at_z(d), device_id_type=MESH)
+    for to in (other, corner):
+        pl.semaphore_signal(barrier, 1, device_id=to, device_id_type=MESH)
+    for c in loads[1:]:
         c.start()
-    barrier = pltpu.get_barrier_semaphore()
-
-    def greet(k, _):
-        pl.semaphore_signal(barrier, 1, device_id=(peer_of(k), batch), device_id_type=MESH)
-        return 0
-
-    lax.fori_loop(1, 64, greet, 0)
-    pl.semaphore_signal(barrier, 1, device_id=other, device_id_type=MESH)
-    pl.semaphore_signal(barrier, 1, device_id=corner, device_id_type=MESH)
-    for d in (1, 3, 5, 7):
-        pl.semaphore_signal(barrier, 1, device_id=at_z(d), device_id_type=MESH)
 
     fill = one_hot(128, 128, lambda o: ((o >> 2) & 1) * 64 + (o >> 3) * 4 + (o & 3))
 
@@ -137,12 +133,14 @@
 
     loads[0].wait()
     pack(act, 0)
-    pl.semaphore_wait(barrier, 69)
+    pl.semaphore_wait(barrier, 24)
+    for d in (2, 4, 6):
+        pl.semaphore_signal(plane_in, 1, device_id=at_z(d), device_id_type=MESH)
+    pl.semaphore_wait(plane_in, 3)
     for g in range(3):
         push(g, send.at[0], recv.at[0], a2a_s.at[0], a2a_r.at[0])
     loads[1].wait()
     pack(cot, 1)
-    arrive(0, recv.at[0], a2a_r.at[0])
     for g in range(3):
         push(g, send.at[1], recv.at[1], a2a_s.at[1], a2a_r.at[1])
 
@@ -157,6 +155,7 @@
                 dst[rows, :384] = out[t * 16 : t * 16 + 16]
                 dst[rows, 384:] = out[64 + t * 16 : 64 + t * 16 + 16]
 
+    arrive(0, recv.at[0], a2a_r.at[0])
     arrive(2, recv.at[0], a2a_r.at[0])
     arrive(1, recv.at[0], a2a_r.at[0])
     unpack(0, x_ref)
@@ -223,8 +222,13 @@
     gm[...] = dot(c_ref[...], wout[...], 1, 1).astype(BF)
     for it in batches:
         gs = [spread(t) for t in take(gm, 0, it)]
-        p = [prob[c * PAIRS + h].astype(BF) for c, h in it]
-        put(gp.at[2], it, [dot(a, b).astype(BF) for a, b in zip(p, gs)])
+        dp = [dot(v, g, 1, 1) for v, g in zip(take(proj, 1536, it), gs)]
+        p = [prob[c * PAIRS + h] for c, h in it]
+        put(gp.at[2], it, [dot(a.astype(BF), g).astype(BF) for a, g in zip(p, gs)])
+        ds = [(a * (d - jnp.sum(a * d, axis=0, keepdims=True)) * scale).astype(BF) for a, d in zip(p, dp)]
+        put(gp.at[0], it, [gather(dot(d, k, 0, 0)).astype(BF) for d, k in zip(ds, take(proj, 768, it))])
+        qs = [spread(t) for t in take(proj, 0, it)]
+        put(gp.at[1], it, [dot(d, q).astype(BF) for d, q in zip(ds, qs)])
 
     def share(s):
         cp = remote(gp.at[s, :, their_c], gfull.at[s, half], fac_s.at[4 + s], fac_r.at[4 + s], other)
@@ -233,6 +237,8 @@
         return cp
 
     fv = share(2)
+    fq = share(0)
+    fk = share(1)
 
     def first_axis(m):
         return (x, at_x) if m % 2 == 0 else (y, at_y)
@@ -243,41 +249,60 @@
     def block(pos, part):
         return pl.ds(pl.multiple_of((pos % 4) * 192 + part * 96, 96), 96)
 
+    def slot(m, i):
+        return ring.at[m, i // 2, pl.ds((i % 2) * 96, 96)]
+
     def ring_copy(m, i, src, to):
-        return remote(src, ring.at[m, i], ring_s.at[m, i], ring_r.at[m, i], to)
+        return remote(src, slot(m, i), ring_s.at[m, i], ring_r.at[m, i], to)
 
     def ring_start(m):
         pos, to = first_axis(m)
         g = grad.at[m]
-        cps = [
-            ring_copy(m, 0, g.at[block(pos + 2, 0)], to(1)),
-            ring_copy(m, 1, g.at[block(pos + 2, 1)], to(3)),
-            ring_copy(m, 2, g.at[block(pos + 3, 0)], to(3)),
-            ring_copy(m, 3, g.at[block(pos + 1, 1)], to(1)),
-        ]
+        if m in DIRECT:
+            cps = []
+            for d in (2, 1, 3):
+                src = g.at[pl.ds(pl.multiple_of((pos + d) % 4 * 192, 192), 192)]
+                cps.append(remote(src, ring.at[m, d - 1], ring_s.at[m, d - 1], ring_r.at[m, d - 1], to(d)))
+        else:
+            cps = [
+                ring_copy(m, 0, g.at[block(pos + 2, 0)], to(1)),
+                ring_copy(m, 1, g.at[block(pos + 2, 1)], to(3)),
+                ring_copy(m, 2, g.at[block(pos + 3, 0)], to(3)),
+                ring_copy(m, 3, g.at[block(pos + 1, 1)], to(1)),
+            ]
         for c in cps:
             c.start()
         return cps
 
     def ring_pass(m, cps):
+        if m in DIRECT:
+            return
         pos, to = first_axis(m)
         cps[0].wait_recv()
         b = block(pos + 1, 0)
-        grad[m, b] = (grad[m, b].astype(F32) + ring[m, 0].astype(F32)).astype(BF)
+        grad[m, b] = (grad[m, b].astype(F32) + slot(m, 0)[...].astype(F32)).astype(BF)
         cps.append(ring_copy(m, 4, grad.at[m, b], to(1)))
         cps[4].start()
         cps[1].wait_recv()
         b = block(pos + 3, 1)
-        grad[m, b] = (grad[m, b].astype(F32) + ring[m, 1].astype(F32)).astype(BF)
+        grad[m, b] = (grad[m, b].astype(F32) + slot(m, 1)[...].astype(F32)).astype(BF)
         cps.append(ring_copy(m, 5, grad.at[m, b], to(3)))
         cps[5].start()
 
     def ring_end(m, cps):
         pos, _ = first_axis(m)
+        if m in DIRECT:
+            for c in cps:
+                c.wait_recv()
+            t = grad[m, pl.ds(pl.multiple_of(pos * 192, 192), 192)].astype(F32)
+            for d in range(3):
+                t = t + ring[m, d].astype(F32)
+            summed[m] = t.astype(BF)
+            return
         for c in cps[2:]:
             c.wait_recv()
         for part, i, j in ((0, 2, 4), (1, 3, 5)):
-            t = grad[m, block(pos, part)].astype(F32) + ring[m, i].astype(F32) + ring[m, j].astype(F32)
+            t = grad[m, block(pos, part)].astype(F32) + slot(m, i)[...].astype(F32) + slot(m, j)[...].astype(F32)
             summed[m, pl.ds(part * 96, 96)] = t.astype(BF)
 
     def row48(pos):
@@ -338,18 +363,6 @@
     fv.wait_recv()
     grad[1] = dot(nfy[...], gfull[2]).astype(BF)
     r1 = ring_start(1)
-    for it in batches:
-        gs = [spread(t) for t in take(gm, 0, it)]
-        dp = [dot(v, g, 1, 1) for v, g in zip(take(proj, 1536, it), gs)]
-        p = [prob[c * PAIRS + h] for c, h in it]
-        ds = [(a * (d - jnp.sum(a * d, axis=0, keepdims=True)) * scale).astype(BF) for a, d in zip(p, dp)]
-        put(gp.at[0], it, [gather(dot(d, k, 0, 0)).astype(BF) for d, k in zip(ds, take(proj, 768, it))])
-        qs = [spread(t) for t in take(proj, 0, it)]
-        put(gp.at[1], it, [dot(d, q).astype(BF) for d, q in zip(ds, qs)])
-    fq = share(0)
-    fk = share(1)
-    ring_pass(0, r0)
-    ring_pass(1, r1)
     fx.wait_recv()
     fq.wait_recv()
     grad[2] = dot(nfx[...], gfull[0]).astype(BF)
@@ -357,6 +370,8 @@
     fk.wait_recv()
     grad[3] = dot(nfy[...], gfull[1]).astype(BF)
     r3 = ring_start(3)
+    ring_pass(0, r0)
+    ring_pass(1, r1)
     gn = dot(gp[0], wqkv[:, :768], 1, 1) + dot(gp[1], wqkv[:, 768:1536], 1, 1) + dot(gp[2], wqkv[:, 1536:], 1, 1)
     xf = x_ref[...].astype(F32)
     centre = jnp.mean(gn * xf, axis=-1, keepdims=True)
@@ -491,12 +506,13 @@
             vm((512, 384), BF),
             vm((3, 512, 384), BF),
             vm((4, 768, 384), BF),
-            vm((4, 6, 96, 384), BF),
+            vm((4, 3, 192, 384), BF),
             vm((4, 192, 384), BF),
             vm((4, 3, 48, 384), BF),
             vm((4, 4, 16, 384), BF),
             vm((2, 8, 16, 384), BF),
             vm((2, 4, 16, 384), BF),
+            pltpu.SemaphoreType.REGULAR,
             dma((6,)),
             dma((3, 3)),
             dma((3, 3)),

time: 74.1 us -> 71.8 us (0.969)
  Pallas kernels: 73.4 us -> 71 us
    pallas_call x1, Pallas kernels: 71.5 us -> 69.2 us  [local(): pl.pallas_call(body, out_shape=(jax.ShapeDtypeStruct((256, 768), BF), jax...]
where the time goes in v3:
time: 71.8 us; the launch traced here: 71.7 us
  Pallas kernels  71 us (99%)
    pallas_call x1, Pallas kernels, local(): pl.pallas_call(body, out_shape=(jax.ShapeDtypeStruct((256, 768), BF), jax...  69.2 us
    pallas_call x1, Pallas kernels, local(): pl.pallas_call(hand_over, out_shape=tuple((jax.ShapeDtypeStruct(v.shape,...  1.85 us

profile of v3, /device:TPU:1, one launch (start us, length us, event | category | flops | bytes accessed | tf_op | source)
XLA Modules:
  0.0 71.7 jit_solution(8181134727402368812)
XLA Ops:
  0.6 69.2 %column_backward.1 = (bf16[256,768]{1,0:T(8,128)(2,1)}, f32[12,2304]{1,0:T(8,128)}, f32[12,768]{1,0:T(8,128)}) custom-call(bf16[256,768]{1,0:T(8,128)(2,1)} %bitcast.3, bf16[256,768]{1,0:T(8,128)(2,1)} %bitcast.4, bf16[768,2304]{1,0:T(8,128)(2,1)} %wqkv_hbm.1, bf16[768,768]{1,0:T(8,128)(2,1)} %wout_hbm.1, bf16[768,768]{1,0:T(8,128)(2,1)} %constant.4.clone.ordx_hbm, ...), custom_call_target="tpu_custom_call" | custom-call | tf_op jit(solution)/shard_map/column_backward/pallas_call | solution.py:471
  69.8 1.8 %hand_over.1 = (bf16[256,768]{1,0:T(8,128)(2,1)}, f32[12,2304]{1,0:T(8,128)}, f32[12,768]{1,0:T(8,128)}) custom-call(bf16[256,768]{1,0:T(8,128)(2,1)} %get-tuple-element.9.a, f32[12,2304]{1,0:T(8,128)} %get-tuple-element.10.b, f32[12,768]{1,0:T(8,128)} %get-tuple-element.11.c), custom_call_target="tpu_custom_call" | custom-call | tf_op jit(solution)/shard_map/hand_over/pallas_call | solution.py:533

commit v4 on v3

--- a/solution.py
+++ b/solution.py
@@ -17,7 +17,6 @@
 GROUP = 4
 WIDE = GROUP * HD
 PAIRS = HEADS // GROUP
-DIRECT = ()
 BATCH = 6
 
 
@@ -96,7 +95,7 @@
 
     def push(group, src, dst, s, r):
         def one(dz, k):
-            peer = ((y + k // 4) % 4) * 16 + ((zh + dz) % 4) * 4 + (x + k % 4) % 4
+            peer = ((y + k % 4) % 4) * 16 + ((zh + dz) % 4) * 4 + (x + k // 4) % 4
             pltpu.make_async_remote_copy(
                 src_ref=src.at[peer],
                 dst_ref=dst.at[band],
@@ -131,11 +130,11 @@
         n = (16, 32, 15)[group]
         pltpu.make_async_copy(dst.at[pl.ds(0, n)], dst.at[pl.ds(0, n)], sem.at[group]).wait()
 
-    loads[0].wait()
-    pack(act, 0)
     pl.semaphore_wait(barrier, 24)
     for d in (2, 4, 6):
         pl.semaphore_signal(plane_in, 1, device_id=at_z(d), device_id_type=MESH)
+    loads[0].wait()
+    pack(act, 0)
     pl.semaphore_wait(plane_in, 3)
     for g in range(3):
         push(g, send.at[0], recv.at[0], a2a_s.at[0], a2a_r.at[0])
@@ -258,25 +257,21 @@
     def ring_start(m):
         pos, to = first_axis(m)
         g = grad.at[m]
-        if m in DIRECT:
-            cps = []
-            for d in (2, 1, 3):
-                src = g.at[pl.ds(pl.multiple_of((pos + d) % 4 * 192, 192), 192)]
-                cps.append(remote(src, ring.at[m, d - 1], ring_s.at[m, d - 1], ring_r.at[m, d - 1], to(d)))
-        else:
-            cps = [
-                ring_copy(m, 0, g.at[block(pos + 2, 0)], to(1)),
-                ring_copy(m, 1, g.at[block(pos + 2, 1)], to(3)),
-                ring_copy(m, 2, g.at[block(pos + 3, 0)], to(3)),
-                ring_copy(m, 3, g.at[block(pos + 1, 1)], to(1)),
-            ]
-        for c in cps:
+        cps = [
+            ring_copy(m, 0, g.at[block(pos + 2, 0)], to(1)),
+            ring_copy(m, 1, g.at[block(pos + 2, 1)], to(3)),
+            ring_copy(m, 2, g.at[block(pos + 3, 0)], to(3)),
+            ring_copy(m, 3, g.at[block(pos + 1, 1)], to(1)),
+        ]
+        for c in cps[:2]:
             c.start()
         return cps
 
+    def ring_near(cps):
+        for c in cps[2:]:
+            c.start()
+
     def ring_pass(m, cps):
-        if m in DIRECT:
-            return
         pos, to = first_axis(m)
         cps[0].wait_recv()
         b = block(pos + 1, 0)
@@ -291,14 +286,6 @@
 
     def ring_end(m, cps):
         pos, _ = first_axis(m)
-        if m in DIRECT:
-            for c in cps:
-                c.wait_recv()
-            t = grad[m, pl.ds(pl.multiple_of(pos * 192, 192), 192)].astype(F32)
-            for d in range(3):
-                t = t + ring[m, d].astype(F32)
-            summed[m] = t.astype(BF)
-            return
         for c in cps[2:]:
             c.wait_recv()
         for part, i, j in ((0, 2, 4), (1, 3, 5)):
@@ -370,8 +357,12 @@
     fk.wait_recv()
     grad[3] = dot(nfy[...], gfull[1]).astype(BF)
     r3 = ring_start(3)
+    ring_near(r0)
+    ring_near(r1)
     ring_pass(0, r0)
     ring_pass(1, r1)
+    ring_near(r2)
+    ring_near(r3)
     gn = dot(gp[0], wqkv[:, :768], 1, 1) + dot(gp[1], wqkv[:, 768:1536], 1, 1) + dot(gp[2], wqkv[:, 1536:], 1, 1)
     xf = x_ref[...].astype(F32)
     centre = jnp.mean(gn * xf, axis=-1, keepdims=True)
@@ -402,6 +393,11 @@
     second_end(3, s3)
     z1 = z_start(1)
     e0 = z_end(0, z0)
+    for c in [fx, fy, fm, fc, fv, fq, fk] + r0 + r1 + r2 + r3 + s0 + s1 + s2 + s3:
+        c.wait_send()
+    for g in range(3):
+        arrive(g, send.at[0], a2a_s.at[0])
+        arrive(g, send.at[1], a2a_s.at[1])
     for g in range(3):
         arrive(g, brecv, a2a_r.at[2])
     home = one_hot(128, 128, lambda o: (((o & 63) >> 2) << 3) + ((o >> 6) << 2) + (o & 3))
@@ -416,6 +412,10 @@
     ]
     outs[0].start()
     e1 = z_end(1, z1)
+    for g in range(3):
+        arrive(g, bsend, a2a_s.at[2])
+    for c in z0 + e0:
+        c.wait_send()
     for pair, cps in ((0, e0), (1, e1)):
         for c in cps:
             c.wait_recv()
@@ -424,14 +424,9 @@
             at = (0, 1536, 0, 768)[m] + (q % 2) * 384
             dst = gout_ref if m == 0 else gqkv_ref
             dst[:, at : at + 384] = fin[pair, q].astype(F32)[:12]
-    outs[1].start()
-    outs[2].start()
-    for c in [fx, fy, fm, fc, fv, fq, fk] + r0 + r1 + r2 + r3 + s0 + s1 + s2 + s3 + z0 + z1 + e0 + e1:
+        outs[2 - pair].start()
+    for c in z1 + e1:
         c.wait_send()
-    for g in range(3):
-        arrive(g, send.at[0], a2a_s.at[0])
-        arrive(g, send.at[1], a2a_s.at[1])
-        arrive(g, bsend, a2a_s.at[2])
     for c in outs:
         c.wait()
 

time: 71.8 us -> 70.7 us (0.985)
  Pallas kernels: 71 us -> 69.9 us
    pallas_call x1, Pallas kernels: 69.2 us -> 68.1 us  [local(): pl.pallas_call(body, out_shape=(jax.ShapeDtypeStruct((256, 768), BF), jax...]
where the time goes in v4:
time: 70.7 us; the launch traced here: 70.5 us
  Pallas kernels  69.9 us (99%)
    pallas_call x1, Pallas kernels, local(): pl.pallas_call(body, out_shape=(jax.ShapeDtypeStruct((256, 768), BF), jax...  68.1 us
    pallas_call x1, Pallas kernels, local(): pl.pallas_call(hand_over, out_shape=tuple((jax.ShapeDtypeStruct(v.shape,...  1.85 us

profile of v4, /device:TPU:1, one launch (start us, length us, event | category | flops | bytes accessed | tf_op | source)
XLA Modules:
  0.0 70.5 jit_solution(3416638784103409106)
XLA Ops:
  0.6 68.1 %column_backward.1 = (bf16[256,768]{1,0:T(8,128)(2,1)}, f32[12,2304]{1,0:T(8,128)}, f32[12,768]{1,0:T(8,128)}) custom-call(bf16[256,768]{1,0:T(8,128)(2,1)} %bitcast.3, bf16[256,768]{1,0:T(8,128)(2,1)} %bitcast.4, bf16[768,2304]{1,0:T(8,128)(2,1)} %wqkv_hbm.1, bf16[768,768]{1,0:T(8,128)(2,1)} %wout_hbm.1, bf16[768,768]{1,0:T(8,128)(2,1)} %constant.4.clone.ordx_hbm, ...), custom_call_target="tpu_custom_call" | custom-call | tf_op jit(solution)/shard_map/column_backward/pallas_call | solution.py:466
  68.7 1.8 %hand_over.1 = (bf16[256,768]{1,0:T(8,128)(2,1)}, f32[12,2304]{1,0:T(8,128)}, f32[12,768]{1,0:T(8,128)}) custom-call(bf16[256,768]{1,0:T(8,128)(2,1)} %get-tuple-element.9.a, f32[12,2304]{1,0:T(8,128)} %get-tuple-element.10.b, f32[12,768]{1,0:T(8,128)} %get-tuple-element.11.c), custom_call_target="tpu_custom_call" | custom-call | tf_op jit(solution)/shard_map/hand_over/pallas_call | solution.py:528

commit v5 on v4

--- a/solution.py
+++ b/solution.py
@@ -219,7 +219,21 @@
     fc.start()
     cfull[half] = c_ref[:, own_c]
     gm[...] = dot(c_ref[...], wout[...], 1, 1).astype(BF)
-    for it in batches:
+    def share(n):
+        out = []
+        for s in (2, 0, 1):
+            rows = pl.ds(n * 128, 128)
+            into = pl.ds(pl.multiple_of(core * 256 + n * 128, 128), 128)
+            cp = remote(
+                gp.at[s, rows, their_c], gfull.at[s, into], fac_s.at[4 + s * 2 + n], fac_r.at[4 + s * 2 + n], other
+            )
+            cp.start()
+            gfull[s, into] = gp[s, rows, own_c]
+            out.append(cp)
+        return out
+
+    shared = []
+    for n, it in enumerate(batches):
         gs = [spread(t) for t in take(gm, 0, it)]
         dp = [dot(v, g, 1, 1) for v, g in zip(take(proj, 1536, it), gs)]
         p = [prob[c * PAIRS + h] for c, h in it]
@@ -228,16 +242,8 @@
         put(gp.at[0], it, [gather(dot(d, k, 0, 0)).astype(BF) for d, k in zip(ds, take(proj, 768, it))])
         qs = [spread(t) for t in take(proj, 0, it)]
         put(gp.at[1], it, [dot(d, q).astype(BF) for d, q in zip(ds, qs)])
-
-    def share(s):
-        cp = remote(gp.at[s, :, their_c], gfull.at[s, half], fac_s.at[4 + s], fac_r.at[4 + s], other)
-        cp.start()
-        gfull[s, half] = gp[s, :, own_c]
-        return cp
-
-    fv = share(2)
-    fq = share(0)
-    fk = share(1)
+        shared.append(share(n))
+    fv, fq, fk = [[a, b] for a, b in zip(*shared)]
 
     def first_axis(m):
         return (x, at_x) if m % 2 == 0 else (y, at_y)
@@ -347,14 +353,17 @@
     grad[0] = dot(mfx[...], cfull[...]).astype(BF)
     r0 = ring_start(0)
     fy.wait_recv()
-    fv.wait_recv()
+    for c in fv:
+        c.wait_recv()
     grad[1] = dot(nfy[...], gfull[2]).astype(BF)
     r1 = ring_start(1)
     fx.wait_recv()
-    fq.wait_recv()
+    for c in fq:
+        c.wait_recv()
     grad[2] = dot(nfx[...], gfull[0]).astype(BF)
     r2 = ring_start(2)
-    fk.wait_recv()
+    for c in fk:
+        c.wait_recv()
     grad[3] = dot(nfy[...], gfull[1]).astype(BF)
     r3 = ring_start(3)
     ring_near(r0)
@@ -393,7 +402,7 @@
     second_end(3, s3)
     z1 = z_start(1)
     e0 = z_end(0, z0)
-    for c in [fx, fy, fm, fc, fv, fq, fk] + r0 + r1 + r2 + r3 + s0 + s1 + s2 + s3:
+    for c in [fx, fy, fm, fc] + fv + fq + fk + r0 + r1 + r2 + r3 + s0 + s1 + s2 + s3:
         c.wait_send()
     for g in range(3):
         arrive(g, send.at[0], a2a_s.at[0])
@@ -511,8 +520,8 @@
             dma((6,)),
             dma((3, 3)),
             dma((3, 3)),
-            dma((7,)),
-            dma((7,)),
+            dma((10,)),
+            dma((10,)),
             dma((4, 6)),
             dma((4, 6)),
             dma((4, 3)),

time: 70.7 us -> 70.7 us (level)
  no operation moved by 1% of the time
where the time goes in v5:
time: 70.7 us; the launch traced here: 70.6 us
  Pallas kernels  70 us (99%)
    pallas_call x1, Pallas kernels, local(): pl.pallas_call(body, out_shape=(jax.ShapeDtypeStruct((256, 768), BF), jax...  68.1 us
    pallas_call x1, Pallas kernels, local(): pl.pallas_call(hand_over, out_shape=tuple((jax.ShapeDtypeStruct(v.shape,...  1.85 us

profile of v5, /device:TPU:1, one launch (start us, length us, event | category | flops | bytes accessed | tf_op | source)
XLA Modules:
  0.0 70.6 jit_solution(15425297264542460300)
XLA Ops:
  0.6 68.1 %column_backward.1 = (bf16[256,768]{1,0:T(8,128)(2,1)}, f32[12,2304]{1,0:T(8,128)}, f32[12,768]{1,0:T(8,128)}) custom-call(bf16[256,768]{1,0:T(8,128)(2,1)} %bitcast.3, bf16[256,768]{1,0:T(8,128)(2,1)} %bitcast.4, bf16[768,2304]{1,0:T(8,128)(2,1)} %wqkv_hbm.1, bf16[768,768]{1,0:T(8,128)(2,1)} %wout_hbm.1, bf16[768,768]{1,0:T(8,128)(2,1)} %constant.4.clone.ordx_hbm, ...), custom_call_target="tpu_custom_call" | custom-call | tf_op jit(solution)/shard_map/column_backward/pallas_call | solution.py:475
  68.7 1.8 %hand_over.1 = (bf16[256,768]{1,0:T(8,128)(2,1)}, f32[12,2304]{1,0:T(8,128)}, f32[12,768]{1,0:T(8,128)}) custom-call(bf16[256,768]{1,0:T(8,128)(2,1)} %get-tuple-element.9.a, f32[12,2304]{1,0:T(8,128)} %get-tuple-element.10.b, f32[12,768]{1,0:T(8,128)} %get-tuple-element.11.c), custom_call_target="tpu_custom_call" | custom-call | tf_op jit(solution)/shard_map/hand_over/pallas_call | solution.py:537
